TPU v7x, 512 devices: a whole 4x4x16 slice. The times are simulated.
512 devices in a mesh: blk: 128 (over z, y, x_lo), vox: 4 (over x_hi, core).
Axes of the slice: x: 4 (x_hi: 2, x_lo: 2; x = x_hi * 2 + x_lo), y: 4, z: 16, core: 2. Of those that a mesh axis runs over, the one named last changes fastest.
Arguments:
- particles: bfloat16 [24576, 2, 5120], P('blk', None, 'vox'), may hold values from -6 to 6
- classes: int32 [24576], P('blk'), may hold values from 0 to 7
- plan: int32 [2, 128], replicated, may hold values from 0 to 127, as said below
- voxel_shell: int32 [5120], P('vox'), may hold values from 4 to 16
- voxel_angle: int32 [5120], P('vox'), may hold values from 0 to 89
- shell_gain: float32 [13], replicated, may hold values from 0.25 to 4
Outputs:
- significance: float32 [3, 24576, 192], P(None, 'blk', 'vox')
Inputs may be any that keep to these rules, and one draw needn't show every extreme that they name: In round r every block b meets block plan[r, b] = b XOR 2^k, with one k a round and different k in different rounds; every block is its partner's partner.
All inputs are finite; a program needn't handle non-finite values.
Results may differ from a plain program's by a relative error of at most 0.0013.
Values may be sent and summed in bfloat16 or wider, within the bound.
No kernel may reach another device: no remote copies, remote signals or barrier semaphores. Data moves between devices by JAX's collectives and lax.ppermute only.
A program may use at most 64 MiB of HBM per device.

v0:
```python
import math

import jax
import jax.numpy as jnp
from jax import lax
from jax.sharding import PartitionSpec as P

first_shell = 4
epsilon = 1e-05


def as_sent(shard):

    def short(part):
        return part.astype(jnp.bfloat16) if part.dtype == jnp.float32 else part

    return jax.tree.map(short, shard)


def swapped(shard, axis, bit):
    return lax.ppermute(shard, axis, [(i, i ^ 1 << bit) for i in range(lax.axis_size(axis))])


def tables(voxel_shell, voxel_angle, shell_gain):
    limits = 48 + 3 * jnp.arange(8, dtype=jnp.int32)
    mask_table = (voxel_angle[None, :] <= limits[:, None]).astype(jnp.float32)
    shells = first_shell + jnp.arange(shell_gain.shape[0], dtype=jnp.int32)
    weights = jnp.sum(
        jnp.where(voxel_shell[None, :] == shells[:, None], shell_gain[:, None], jnp.float32(0.0)),
        axis=0,
    )
    weight_table = (mask_table * weights[None, :]).astype(jnp.bfloat16)
    return (mask_table, weight_table)


def contract(left_side, right_side):
    return lax.dot_general(
        left_side, right_side, (((1,), (1,)), ((), ())), preferred_element_type=jnp.float32
    )


def onehot_rows(labels_in, dtype):
    labels = jnp.arange(8, dtype=jnp.int32)
    return (labels_in[..., None] == labels).astype(dtype)


def prepare(block, block_classes, mask_table, weight_table):
    row_count = block.shape[0]
    onehot = onehot_rows(block_classes, jnp.bfloat16)
    row_mask = jnp.dot(onehot, mask_table.astype(jnp.bfloat16), preferred_element_type=jnp.float32)
    row_weights = jnp.dot(onehot, weight_table, preferred_element_type=jnp.float32)
    widened = block.astype(jnp.float32)
    masked = (widened * row_mask[:, None, :]).astype(jnp.bfloat16).reshape(row_count, -1)
    weighted = (widened * row_weights[:, None, :]).astype(jnp.bfloat16).reshape(row_count, -1)
    power_rows = (jnp.sum(widened * widened, axis=1) * row_mask).astype(jnp.bfloat16)
    return (masked, weighted, power_rows, row_weights.astype(jnp.bfloat16))


def partials(own_prep, other_prep):
    score_sum = contract(own_prep[0], other_prep[1])
    return (score_sum, contract(own_prep[2], other_prep[3]), contract(own_prep[3], other_prep[2]))


def finish(stacked, voxel_total):
    score_sum, left_norm, right_norm = lax.psum_scatter(
        stacked, "vox", scatter_dimension=2, tiled=True
    )
    return (
        score_sum
        / math.sqrt(voxel_total)
        * lax.rsqrt((left_norm / voxel_total + epsilon) * (right_norm / voxel_total + epsilon))
    )


def fetch_block(payload, mask_value, bit_count):
    for bit_number in range(bit_count):
        payload = lax.cond(
            mask_value == 1 << bit_number,
            lambda carried: jax.tree.map(
                lambda part, own: part.astype(own.dtype),
                swapped(as_sent(carried), "blk", bit_number),
                carried,
            ),
            lambda carried: carried,
            payload,
        )
    return payload


def body(particles, classes, plan, voxel_shell, voxel_angle, shell_gain):
    voxel_total = particles.shape[2] * lax.axis_size("vox")
    mask_table, weight_table = tables(voxel_shell, voxel_angle, shell_gain)
    own_prep = prepare(particles, classes, mask_table, weight_table)
    bit_count = lax.axis_size("blk").bit_length() - 1
    slot_parts = [partials(own_prep, own_prep)]
    slot_classes = [classes]
    for round_index in range(plan.shape[0]):
        block, block_classes = fetch_block((particles, classes), plan[round_index, 0], bit_count)
        other_prep = prepare(block, block_classes, mask_table, weight_table)
        slot_parts.append(partials(own_prep, other_prep))
        slot_classes.append(block_classes)
    pieces = [
        finish(tuple((member[None] for member in parts_now)), voxel_total)
        for parts_now in slot_parts
    ]
    return jnp.concatenate(pieces, axis=0)


def solution(mesh):
    in_specs = (P("blk", None, "vox"), P("blk"), P(), P("vox"), P("vox"), P())
    out_specs = P(None, "blk", "vox")
    return jax.shard_map(body, mesh=mesh, in_specs=in_specs, out_specs=out_specs, check_vma=False)
```

profile of v0, /device:TPU:1, one launch (start us, length us, event | category | flops | bytes accessed | tf_op | source)
XLA Modules:
  0.0 266.4 jit_solution(6406725101084466008)
XLA Ops:
  6.6 1.3 fusion.81
  16.9 0.8 select_reduce_fusion
  17.7 1.0 fusion.22
  18.7 0.0 copy-start
  18.7 0.3 fusion.82
  19.1 0.9 copy-done
  19.9 5.2 %fusion.3 = (bf16[192,2,1280]{2,1,0:T(2,128)(2,1)}, f32[192,1280]{1,0:T(8,128)S(1)}, bf16[192,2,1280]{2,1,0:T(2,128)(2,1)}) fusion(bf16[192,2,1280]{2,1,0:T(2,128)(2,1)S(1)} %copy-done, f32[192,1280]{1,0:T(8,128)S(1)} %get-tuple-element.212, f32[192,1280]{1,0:T(8,128)S(1)} %fusion.22), kind=kLoop, calls=%fused_computation.12 | loop fusion | flops 3194880 | bytes 5898240 | tf_op jit(solution)/shard_map/convert_element_type | solution.py:54
  25.2 0.1 multiply_convert_fusion
  25.3 0.3 convolution_bitcast_fusion.2
  25.6 0.3 convolution_bitcast_fusion.3
  25.9 1.5 conditional.33
  25.9 1.0 copy.133
  26.9 0.6 copy.134
  27.5 95.5 %conditional.38 = ((bf16[192,2,1280]{2,1,0:T(2,128)(2,1)}, s32[192]{0:T(256)})) conditional(s32[]{:T(128)} %bitcast.16, (bf16[192,2,1280]{2,1,0:T(2,128)(2,1)}, s32[192]{0:T(256)}) %get-tuple-element.298, (bf16[192,2,1280]{2,1,0:T(2,128)(2,1)}, s32[192]{0:T(256)}) %get-tuple-element.298), branch_computations={%region_33.34_spmd, %region_34.35_spmd} | conditional | bytes 5902952 | solution.py:77
  27.5 9.6 %collective-permute-start.22 = (bf16[192,2,1280]{2,1,0:T(2,128)(2,1)}, bf16[192,2,1280]{2,1,0:T(2,128)(2,1)S(1)}, u32[]{:S(2)}, u32[]{:S(2)}) collective-permute-start(bf16[192,2,1280]{2,1,0:T(2,128)(2,1)} %get-tuple-element.161), channel_id=1, source_target_pairs={{0,128},{4,132},{8,136},{12,140},{16,144},{20,148},{24,152},{28,15... | collective-permute-start | bytes 2949128 | tf_op jit(solution)/shard_map/cond/branch_1_fun/ppermute | solution.py:21
  37.1 1.9 collective-permute-start.23
  39.0 82.3 %collective-permute-done.23 = s32[192]{0:T(256)S(1)} collective-permute-done((s32[192]{0:T(256)}, s32[192]{0:T(256)S(1)}, u32[]{:S(2)}, u32[]{:S(2)}) %collective-permute-start.23) | collective-permute-done | bytes 800 | tf_op jit(solution)/shard_map/cond/branch_1_fun/ppermute | solution.py:21
  121.4 0.6 copy.156
  121.9 1.0 copy.155
  122.9 4.0 %conditional.41 = (s32[192]{0:T(256)}, bf16[192,2,1280]{2,1,0:T(2,128)(2,1)}, f32[192,1280]{1,0:T(8,128)S(1)}) conditional(s32[]{:T(128)} %bitcast.15, (s32[192]{0:T(256)}, bf16[192,2,1280]{2,1,0:T(2,128)(2,1)}) %tuple.101, (s32[192]{0:T(256)}, bf16[192,2,1280]{2,1,0:T(2,128)(2,1)}) %tuple.101), branch_computations={%region_35.36_spmd, %region_36.37_spmd} | conditional | flops 1228800 | bytes 7869032
  122.9 3.8 %multiply_reduce_fusion.1 = f32[192,1280]{1,0:T(8,128)S(1)} fusion(bf16[192,2,1280]{2,1,0:T(2,128)(2,1)} %get-tuple-element.246), kind=kLoop, calls=%fused_computation.1 | loop fusion | flops 1228800 | bytes 1966080 | tf_op jit(solution)/shard_map/reduce_sum | solution.py:55
  126.9 0.9 copy-done.1
  127.8 1.0 fusion.19
  128.8 1.8 fusion.10
  130.7 0.8 copy.68
  131.5 0.3 convolution_bitcast_fusion
  131.8 0.8 copy.66
  132.6 2.3 fusion.5
  134.9 0.0 copy-start.7
  134.9 0.5 convolution_bitcast_fusion.4
  135.4 0.8 copy.64
  136.1 1.5 conditional.26
  136.1 1.0 copy.163
  137.1 0.5 copy.164
  137.6 24.9 %conditional.29 = ((bf16[192,2,1280]{2,1,0:T(2,128)(2,1)}, s32[192]{0:T(256)})) conditional(s32[]{:T(128)} %bitcast.7, (bf16[192,2,1280]{2,1,0:T(2,128)(2,1)}, s32[192]{0:T(256)}) %get-tuple-element.291, (bf16[192,2,1280]{2,1,0:T(2,128)(2,1)}, s32[192]{0:T(256)}) %get-tuple-element.291), branch_computations={%region_11.12_spmd, %region_12.13_spmd} | conditional | bytes 5902952 | solution.py:77
  137.6 1.9 collective-permute-start.6
  139.6 3.4 %collective-permute-start.7 = (s32[192]{0:T(256)}, s32[192]{0:T(256)S(1)}, u32[]{:S(2)}, u32[]{:S(2)}) collective-permute-start(s32[192]{0:T(256)} %get-tuple-element.144), channel_id=1, source_target_pairs={{0,32},{4,36},{8,40},{12,44},{16,48},{20,52},{24,56},{28,60},{32,0... | collective-permute-start | bytes 2312 | tf_op jit(solution)/shard_map/cond/branch_1_fun/ppermute | solution.py:21
  142.9 18.1 %collective-permute-done.7 = s32[192]{0:T(256)S(1)} collective-permute-done((s32[192]{0:T(256)}, s32[192]{0:T(256)S(1)}, u32[]{:S(2)}, u32[]{:S(2)}) %collective-permute-start.7) | collective-permute-done | bytes 800 | tf_op jit(solution)/shard_map/cond/branch_1_fun/ppermute | solution.py:21
  161.1 0.5 copy.178
  161.6 0.0 collective-permute-done.6
  161.6 1.0 copy.177
  162.6 4.0 %conditional.40 = (s32[192]{0:T(256)}, bf16[192,2,1280]{2,1,0:T(2,128)(2,1)}, f32[192,1280]{1,0:T(8,128)S(1)}) conditional(s32[]{:T(128)} %bitcast.4, (s32[192]{0:T(256)}, bf16[192,2,1280]{2,1,0:T(2,128)(2,1)}) %tuple.100, (s32[192]{0:T(256)}, bf16[192,2,1280]{2,1,0:T(2,128)(2,1)}) %tuple.100), branch_computations={%region_17.18_spmd, %region_18.19_spmd} | conditional | flops 1228800 | bytes 7869032
  162.6 3.8 %multiply_reduce_fusion = f32[192,1280]{1,0:T(8,128)S(1)} fusion(bf16[192,2,1280]{2,1,0:T(2,128)(2,1)} %get-tuple-element.276), kind=kLoop, calls=%fused_computation | loop fusion | flops 1228800 | bytes 1966080 | tf_op jit(solution)/shard_map/reduce_sum | solution.py:55
  166.6 1.0 fusion.20
  167.6 1.3 fusion.9
  168.8 0.8 copy.60
  169.6 0.3 convolution_bitcast_fusion.1
  169.9 0.8 copy.58
  170.7 2.3 fusion.6
  173.1 0.4 convolution_bitcast_fusion.5
  173.5 0.8 copy.56
  174.3 0.8 copy.52
  175.1 0.8 copy.50
  175.9 0.4 convolution_bitcast_fusion.6
  176.3 0.8 copy.48
  177.1 0.0 all-reduce.12.cloned.1.call-update
  177.2 1.3 dynamic-slice
  179.1 75.5 %all-reduce.12.cloned.1.call-done = (f32[1,192,192]{1,0,2:T(1,128)}, f32[1,192,192]{1,0,2:T(1,128)}, f32[1,192,192]{1,0,2:T(1,128)}, f32[1,192,192]{1,0,2:T(1,12...) async-done(((f32[1,192,192]{1,0,2:T(1,128)}, f32[1,192,192]{1,0,2:T(1,128)}, ...) | async-done | bytes 1327120
  254.6 0.8 constant_dynamic-slice_fusion.8
  255.4 0.8 constant_dynamic-slice_fusion
  256.3 0.8 constant_dynamic-slice_fusion.2
  257.1 0.8 constant_dynamic-slice_fusion.4
  257.9 0.8 constant_dynamic-slice_fusion.6
  258.8 0.7 pad_maximum_fusion
  (27 shorter events, 0.1 us)
Async XLA Ops:
  6.5 12.2 %copy-start.5 = (s32[1280]{0:T(1024)S(1)}, s32[1280]{0:T(1024)}, u32[]{:S(2)}) copy-start(s32[1280]{0:T(1024)} %param.38) | copy-start | bytes 15364
  6.5 12.2 %copy-start.6 = (s32[192]{0:T(256)S(1)}, s32[192]{0:T(256)}, u32[]{:S(2)}) copy-start(s32[192]{0:T(256)} %param.35) | copy-start | bytes 2308
  6.5 248.1 %all-reduce.12.cloned.1.call-start = ((), (), s32[]{:S(2)}) async-start(), calls=%async_computation | async-start | bytes 3538944
  18.7 1.2 copy-start
  27.5 94.5 %collective-permute-start.22 = (bf16[192,2,1280]{2,1,0:T(2,128)(2,1)}, bf16[192,2,1280]{2,1,0:T(2,128)(2,1)S(1)}, u32[]{:S(2)}, u32[]{:S(2)}) collective-permute-start(bf16[192,2,1280]{2,1,0:T(2,128)(2,1)} %get-tuple-element.161), channel_id=1, source_target_pairs={{0,128},{4,132},{8,136},{12,140},{16,144},{20,148},{24,152},{28,15... | collective-permute-start | bytes 2949128 | tf_op jit(solution)/shard_map/cond/branch_1_fun/ppermute | solution.py:21
  37.1 84.3 %collective-permute-start.23 = (s32[192]{0:T(256)}, s32[192]{0:T(256)S(1)}, u32[]{:S(2)}, u32[]{:S(2)}) collective-permute-start(s32[192]{0:T(256)} %get-tuple-element.162), channel_id=1, source_target_pairs={{0,128},{4,132},{8,136},{12,140},{16,144},{20,148},{24,152},{28,15... | collective-permute-start | bytes 2312 | tf_op jit(solution)/shard_map/cond/branch_1_fun/ppermute | solution.py:21
  126.9 0.9 copy-start.1
  132.6 2.3 copy-start.3
  134.9 1.3 copy-start.7
  137.6 24.0 %collective-permute-start.6 = (bf16[192,2,1280]{2,1,0:T(2,128)(2,1)}, bf16[192,2,1280]{2,1,0:T(2,128)(2,1)S(1)}, u32[]{:S(2)}, u32[]{:S(2)}) collective-permute-start(bf16[192,2,1280]{2,1,0:T(2,128)(2,1)} %get-tuple-element.143), channel_id=1, source_target_pairs={{0,32},{4,36},{8,40},{12,44},{16,48},{20,52},{24,56},{28,60},{32,0... | collective-permute-start | bytes 2949128 | tf_op jit(solution)/shard_map/cond/branch_1_fun/ppermute | solution.py:21
  139.6 21.5 %collective-permute-start.7 = (s32[192]{0:T(256)}, s32[192]{0:T(256)S(1)}, u32[]{:S(2)}, u32[]{:S(2)}) collective-permute-start(s32[192]{0:T(256)} %get-tuple-element.144), channel_id=1, source_target_pairs={{0,32},{4,36},{8,40},{12,44},{16,48},{20,52},{24,56},{28,60},{32,0... | collective-permute-start | bytes 2312 | tf_op jit(solution)/shard_map/cond/branch_1_fun/ppermute | solution.py:21
  170.7 2.3 copy-start.4
  173.5 2.4 copy-start.2
Sparse Core Ops, SparseCore 0:
  177.3 77.3 all-reduce.11
where the time goes:
time: 267 us; the launch traced here: 266 us
  waiting for transfers between devices  176 us (66%)
  between operations  23.2 us (9%)
  local copies, waits for them, and re-layouts  21.7 us (8%)
  other arithmetic  19.1 us (7%)
  starting transfers between devices  16.8 us (6%)
  matrix products  8.94 us (3%)
    ppermute x4, waiting for transfers between devices, swapped(): lax.ppermute(shard, axis, [(i, i ^ 1 << bit) for i in range(lax.axis_size...  100 us
    unnamed x2, waiting for transfers between devices  75.6 us
    ppermute x4, starting transfers between devices, swapped(): lax.ppermute(shard, axis, [(i, i ^ 1 << bit) for i in range(lax.axis_size...  16.8 us
    convert_element_type x3, other arithmetic, prepare(): (widened * row_weights[:, None, :]).astype(jnp.bfloat16)  9.84 us
    reduce_sum x2, other arithmetic, prepare(): jnp.sum(widened * widened, axis=1) * row_mask  7.59 us
    unnamed x22, local copies, waits for them, and re-layouts  7.21 us
    broadcast_in_dim x9, local copies, waits for them, and re-layouts, body(): member[None]  7.12 us
    cond x8, local copies, waits for them, and re-layouts  6.07 us
  transfers between devices with their start and end apart: 5, of which 3 were waited for; matrix products, arithmetic and copies ran while one was open for 1% of the time, Pallas kernels for 0%

commit v1 on v0

v1 whole, which is shorter than its diff:
```python
import math

import jax
import jax.numpy as jnp
from jax import lax
from jax.experimental import pallas as pl
from jax.experimental.pallas import tpu as pltpu
from jax.sharding import PartitionSpec as P

first_shell = 4
first_limit = 48
limit_step = 3
class_count = 8
epsilon = 1e-05

f32 = jnp.float32
bf16 = jnp.bfloat16
in_vmem = pl.BlockSpec(memory_space=pltpu.VMEM)
in_smem = pl.BlockSpec(memory_space=pltpu.SMEM)


def shape(dims, dtype):
    return jax.ShapeDtypeStruct(dims, dtype)


def local_call(kernel, out_shape, in_specs, out_specs, args, scratch=()):
    return pl.pallas_call(
        kernel,
        out_shape=out_shape,
        in_specs=in_specs,
        out_specs=out_specs,
        scratch_shapes=scratch,
        compiler_params=pltpu.CompilerParams(vmem_limit_bytes=40 << 20),
    )(*args)


def contract(left_side, right_side):
    return lax.dot_general(
        left_side, right_side, (((1,), (1,)), ((), ())), preferred_element_type=f32
    )


def one_way(blocks, voxes, bit):
    return [
        (b * voxes + v, (b ^ 1 << bit) * voxes + v)
        for b in range(blocks)
        for v in range(voxes)
        if v & 1 == b >> bit & 1
    ]


def back(pairs):
    return [(target, source) for source, target in pairs]


def both_ways(blocks, bit):
    return [(b, b ^ 1 << bit) for b in range(blocks)]


def branch_kernel(bit_count, plan, index_out, flag_out):
    first, second = plan[0, 0], plan[1, 0]

    def bit_of(value):
        return sum([jnp.where(value >= 1 << k, 1, 0) for k in range(1, bit_count)])

    first, second = bit_of(first), bit_of(second)
    low, high = jnp.minimum(first, second), jnp.maximum(first, second)
    index_out[0] = high * (high - 1) // 2 + low
    flag_out[0] = jnp.where(first > second, 1, 0)


def column(row):
    return jnp.broadcast_to(row, (8, row.shape[1])).T[:, 0:1]


def limits_of(labels):
    return first_limit + 1.0 + limit_step * column(labels.astype(f32))


def chunk_of(width):
    return next(size for size in (256, 128, width) if width % size == 0)


def own_kernel(gain, x, labels, shells, angles, left_out, right_out, rows, partial, message, acc):
    chunk = chunk_of(x.shape[2])
    limits = first_limit + limit_step * lax.broadcasted_iota(jnp.int32, (class_count, 1), 0)
    keep_limits = (limits_of(labels[...])).astype(bf16)
    acc[...] = jnp.zeros(acc.shape, f32)
    partial[0:class_count, :] = jnp.zeros((class_count, partial.shape[1]), f32)

    def step(i, carry):
        at = pl.ds(pl.multiple_of(i * chunk, chunk), chunk)
        weights = jnp.zeros((1, chunk), f32)
        for s in range(gain.shape[0]):
            weights = jnp.where(shells[:, at] == s + first_shell, gain[s], weights)
        weights = weights.astype(bf16)
        rows[0:1, at] = weights.astype(f32)
        table = jnp.where(angles[:, at] <= limits, weights.astype(f32), 0.0).astype(bf16)
        keep = jnp.clip(keep_limits - angles[:, at].astype(f32).astype(bf16), 0, 1)
        block = x[:, :, at]
        left = [block[:, t, :] * keep for t in range(2)]
        right = [part * weights for part in left]
        wide = [part.astype(f32) for part in left]
        power = (wide[0] * wide[0] + wide[1] * wide[1]).astype(bf16)
        partial[0:class_count, :] += contract(table, power)
        for t in range(2):
            left_out[t, :, at] = left[t]
            right_out[t, :, at] = right[t]
        acc[...] += contract(right[0], left[0]) + contract(right[1], left[1])
        return carry

    lax.fori_loop(0, x.shape[2] // chunk, step, 0)
    partial[class_count:, :] = jnp.broadcast_to(
        labels[...].astype(f32), (class_count, partial.shape[1])
    )
    parts, height = message.shape[0], message.shape[1] - class_count
    for q in range(parts):
        message[q, 0:height, :] = acc[height * q : height * (q + 1), :]
        message[q, height:, :] = partial[0:class_count, :]


def norms(own_sums, own_labels, slice_sums, slice_labels, total):
    left_norm = jnp.zeros((slice_sums.shape[0], own_sums.shape[1]), f32)
    right_norm = left_norm
    for c in range(class_count):
        left_norm = jnp.where(slice_labels == c, own_sums[c : c + 1, :], left_norm)
        right_norm = jnp.where(own_labels == c, slice_sums[:, c : c + 1], right_norm)
    return lax.rsqrt((left_norm / total + epsilon) * (right_norm / total + epsilon)) / math.sqrt(
        total
    )


def sliced(place, height, sums, labels, scratch):
    scratch[:, 0:class_count] = sums.T
    scratch[:, class_count : 2 * class_count] = jnp.broadcast_to(
        labels, (class_count, labels.shape[1])
    ).T
    part = scratch[pl.ds(pl.multiple_of(place[0] * height, 8), height), :]
    return part[:, 0:class_count], part[:, class_count : class_count + 1]


def summed_of(message):
    summed = message[0]
    for q in range(1, message.shape[0]):
        summed = summed + message[q]
    return summed


def self_kernel(total, place, message, labels, sums_out, out, scratch):
    height = message.shape[1] - class_count
    summed = summed_of(message)
    sums = summed[height:, :]
    sums_out[...] = sums
    own_labels = labels[...].astype(f32)
    slice_sums, slice_labels = sliced(place, height, sums, own_labels, scratch)
    out[...] = summed[0:height, :] * norms(sums, own_labels, slice_sums, slice_labels, total)


def pair_kernel(first, second, rows, left, right, own_out, first_out, second_out, acc):
    chunk = chunk_of(left.shape[2])
    own_out[...] = jnp.zeros(own_out.shape, f32)
    acc[...] = jnp.zeros(acc.shape, f32)

    def step(i, carry):
        at = pl.ds(pl.multiple_of(i * chunk, chunk), chunk)
        weights = rows[0:1, at].astype(bf16)
        for s, block in enumerate((first, second)):
            own_out[s] += contract(block[0, :, at] * weights, left[0, :, at]) + contract(
                block[1, :, at] * weights, left[1, :, at]
            )
            acc[s] += contract(right[0, :, at], block[0, :, at]) + contract(
                right[1, :, at], block[1, :, at]
            )
        return carry

    lax.fori_loop(0, left.shape[2] // chunk, step, 0)
    for s, out in enumerate((first_out, second_out)):
        half, count = out.shape[0], acc.shape[2]
        out[:, 0:count] = acc[s, 0:half, :]
        out[:, count:] = acc[s, half:, :]


def merge_kernel(own, first, second, first_partial, second_partial, out):
    parts, height = out.shape[0], out.shape[1] - class_count
    count = own.shape[2]
    for s, (received, partial) in enumerate(((first, first_partial), (second, second_partial))):
        half = received.shape[0]
        across = slice(count * s, count * (s + 1))
        for q in range(parts):
            side, at = divmod(q * height, half)
            out[q, 0:height, across] = (
                own[s, height * q : height * (q + 1), :]
                + received[at : at + height, count * side : count * (side + 1)]
            )
            out[q, height:, across] = partial[0:class_count, :]


def last_kernel(
    total, flag, place, pieces, sums, labels, first_partial, second_partial, self_out, out, scratch
):
    count, height = out.shape[2], out.shape[1]
    summed = summed_of(pieces)
    own_labels = labels[...].astype(f32)
    out[0] = self_out[...]
    for s, partial in enumerate((first_partial, second_partial)):
        mine = summed[:, count * s : count * (s + 1)]
        slice_sums, slice_labels = sliced(
            place, height, mine[height:, :], partial[class_count : class_count + 1, :], scratch
        )
        out[1 + (s ^ flag[0])] = mine[0:height, :] * norms(
            sums[...], own_labels, slice_sums, slice_labels, total
        )


def body(particles, classes, plan, voxel_shell, voxel_angle, shell_gain):
    blocks, voxes = lax.axis_size("blk"), lax.axis_size("vox")
    bit_count = blocks.bit_length() - 1
    count, _, width = particles.shape
    height, total = count // voxes, width * voxes
    axes = ("blk", "vox")
    bit_pairs = [(low, high) for high in range(bit_count) for low in range(high)]

    def branch_call(*refs):
        branch_kernel(bit_count, *refs)

    def self_call(*refs):
        self_kernel(total, *refs)

    def last_call(*refs):
        last_kernel(total, *refs)

    index, flag = local_call(
        branch_call,
        (shape((1,), jnp.int32), shape((1,), jnp.int32)),
        [in_smem],
        (in_smem, in_smem),
        (plan,),
    )
    index = index[0]
    place = lax.axis_index("vox").reshape(1)
    labels = classes.reshape(1, -1)
    left, right, rows, partial, message = local_call(
        own_kernel,
        (
            shape((2, count, width), bf16),
            shape((2, count, width), bf16),
            shape((8, width), f32),
            shape((2 * class_count, count), f32),
            shape((voxes, height + class_count, count), f32),
        ),
        [in_smem] + [in_vmem] * 4,
        (in_vmem,) * 5,
        (shell_gain, particles, labels, voxel_shell.reshape(1, -1), voxel_angle.reshape(1, -1)),
        [pltpu.VMEM((count, count), f32)],
    )
    message = lax.all_to_all(message, "vox", 0, 0, tiled=True)

    def fetch(bits):
        return lambda block, own_partial: tuple(
            [lax.ppermute(block, axes, one_way(blocks, voxes, bit)) for bit in bits]
            + [lax.ppermute(own_partial, "blk", both_ways(blocks, bit)) for bit in bits]
        )

    def give_back(bits):
        return lambda *sent: tuple(
            lax.ppermute(part, axes, back(one_way(blocks, voxes, bit)))
            for part, bit in zip(sent, bits)
        )

    first, second, first_partial, second_partial = lax.switch(
        index, [fetch(bits) for bits in bit_pairs], left, partial
    )
    scratch = [pltpu.VMEM((count, 2 * class_count), f32)]
    sums, self_out = local_call(
        self_call,
        (shape((class_count, count), f32), shape((height, count), f32)),
        [in_smem, in_vmem, in_vmem],
        (in_vmem, in_vmem),
        (place, message, labels),
        scratch,
    )
    own, first_sent, second_sent = local_call(
        pair_kernel,
        (shape((2, count, count), f32),) + (shape((count // 2, 2 * count), f32),) * 2,
        [in_vmem] * 5,
        (in_vmem,) * 3,
        (first, second, rows, left, right),
        [pltpu.VMEM((2, count, count), f32)],
    )
    first_back, second_back = lax.switch(
        index, [give_back(bits) for bits in bit_pairs], first_sent, second_sent
    )
    merged = local_call(
        merge_kernel,
        shape((voxes, height + class_count, 2 * count), f32),
        [in_vmem] * 5,
        in_vmem,
        (own, first_back, second_back, first_partial, second_partial),
    )
    pieces = lax.all_to_all(merged, "vox", 0, 0, tiled=True)
    out = local_call(
        last_call,
        shape((3, height, count), f32),
        [in_smem, in_smem] + [in_vmem] * 6,
        in_vmem,
        (flag, place, pieces, sums, labels, first_partial, second_partial, self_out),
        scratch,
    )
    return out.transpose(0, 2, 1)


def solution(mesh):
    in_specs = (P("blk", None, "vox"), P("blk"), P(), P("vox"), P("vox"), P())
    out_specs = P(None, "blk", "vox")
    return jax.shard_map(body, mesh=mesh, in_specs=in_specs, out_specs=out_specs, check_vma=False)
```

time: 267 us -> 68 us (0.25)
  waiting for transfers between devices: 176 us -> 12.7 us
  between operations: 23.2 us -> 0.7 us
  starting transfers between devices: 16.8 us -> 36.5 us
  other arithmetic: 19.1 us -> 0 us
  local copies, waits for them, and re-layouts: 21.7 us -> 2.6 us
  Pallas kernels: 0 us -> 14.9 us
  matrix products: 8.94 us -> 0 us
    ppermute x4 -> x6, waiting for transfers between devices: 100 us -> 5.52 us  [the longest x2 4.09 us: fetch(): lax.ppermute(own_partial, 'blk', both_ways(blocks, bit))]
    unnamed x2 -> x0, waiting for transfers between devices: 75.6 us -> none
    all_to_all x0 -> x2, starting transfers between devices: none -> 14.9 us  [the longest x1 10.4 us: body(): message = lax.all_to_all(message, 'vox', 0, 0, tiled=True)]
    pallas_call x0 -> x6, Pallas kernels: none -> 14.9 us  [local_call(): pl.pallas_call(kernel, out_shape=out_shape, in_specs=in_specs, out_specs=...]
    convert_element_type x4 -> x0, other arithmetic: 9.94 us -> none  [the longest x3 9.84 us: prepare(): (widened * row_weights[:, None, :]).astype(jnp.bfloat16)]
    dot_general x13 -> x0, matrix products: 8.94 us -> none  [the longest x9 5.63 us: contract(): lax.dot_general(left_side, right_side, (((1,), (1,)), ((), ())), preferre...]
    reduce_sum x3 -> x0, other arithmetic: 8.41 us -> none  [the longest x2 7.59 us: prepare(): jnp.sum(widened * widened, axis=1) * row_mask]
    all_to_all x0 -> x2, waiting for transfers between devices: none -> 7.15 us  [the longest x1 7.15 us: body(): pieces = lax.all_to_all(merged, 'vox', 0, 0, tiled=True)]
  transfers between devices with their start and end apart: 5 -> 8, of which waited for: 3 -> 4; matrix products, arithmetic and copies ran while one was open for 1% -> 0% of each run, Pallas kernels for 0% -> 10%
where the time goes in v1:
time: 68 us; the launch traced here: 67.4 us
  starting transfers between devices  36.5 us (54%)
  Pallas kernels  14.9 us (22%)
  waiting for transfers between devices  12.7 us (19%)
  local copies, waits for them, and re-layouts  2.6 us (4%)
  between operations  0.7 us (1%)
    pallas_call x6, Pallas kernels, local_call(): pl.pallas_call(kernel, out_shape=out_shape, in_specs=in_specs, out_specs=...  14.9 us
    ppermute x2, starting transfers between devices, fetch(): lax.ppermute(own_partial, 'blk', both_ways(blocks, bit))  11.4 us
    all_to_all x1, starting transfers between devices, body(): message = lax.all_to_all(message, 'vox', 0, 0, tiled=True)  10.4 us
    ppermute x2, starting transfers between devices, give_back(): lax.ppermute(part, axes, back(one_way(blocks, voxes, bit)))  7.62 us
    all_to_all x1, waiting for transfers between devices, body(): pieces = lax.all_to_all(merged, 'vox', 0, 0, tiled=True)  7.15 us
    all_to_all x1, starting transfers between devices, body(): pieces = lax.all_to_all(merged, 'vox', 0, 0, tiled=True)  4.54 us
    ppermute x2, waiting for transfers between devices, fetch(): lax.ppermute(own_partial, 'blk', both_ways(blocks, bit))  4.09 us
    ppermute x2, starting transfers between devices, fetch(): lax.ppermute(block, axes, one_way(blocks, voxes, bit))  2.58 us
  transfers between devices with their start and end apart: 8, of which 4 were waited for; matrix products, arithmetic and copies ran while one was open for 0% of the time, Pallas kernels for 10%

profile of v1, /device:TPU:1, one launch (start us, length us, event | category | flops | bytes accessed | tf_op | source)
XLA Modules:
  0.0 67.4 jit_solution(347953553145162342)
XLA Ops:
  0.0 0.0 copy-start.4
  0.0 0.7 %reshape.17.shells = s32[1,1280]{1,0:T(1,128)S(1)} reshape(s32[1280]{0:T(1024)} %param.51) | data formatting | bytes 10240 | tf_op jit(solution)/shard_map/reshape | solution.py:253
  0.7 0.0 copy-done.4
  0.7 0.0 copy-start.1
  0.7 0.0 copy-start.2
  0.8 0.7 copy-done.1
  1.4 0.0 copy-done.2
  1.4 0.0 copy-start
  1.4 1.2 %copy-done = bf16[192,2,1280]{2,1,0:T(2,128)(2,1)S(1)} copy-done((bf16[192,2,1280]{2,1,0:T(2,128)(2,1)S(1)}, bf16[192,2,1280]{2,1,0:T(2,128)(2,1)}, u32[]{:S(2)}) %copy-start) | copy-done | bytes 983064
  2.6 4.8 %shard_map.65 = (bf16[2,192,1280]{2,1,0:T(8,128)(2,1)S(1)}, bf16[2,192,1280]{2,1,0:T(8,128)(2,1)S(1)}, f32[8,1280]{1,0:T(8,128)S(1)}, f32[16,192]{1,0:T(8,128)S(1)}, f32[4,56,192]{2,1,0:T(8,128)}) custom-call(f32[13]{0:T(128)S(1)} %copy-done.2, bf16[192,2,1280]{2,1,0:T(2,128)(2,1)S(1)} %copy-done, s32[1,192]{1,0:T(1,128)S(1)} %bitcast.4, ...), custom_call_target="tpu_custom_call" | custom-call | tf_op jit(solution)/shard_map/pallas_call | solution.py:27
  7.4 0.0 copy-start.3
  7.4 10.4 %all-to-all-start.1 = ((f32[4,56,192]{2,1,0:T(8,128)}), f32[4,56,192]{2,1,0:T(8,128)S(1)}, u32[]{:S(2)}, u32[]{:S(2)}) async-start(f32[4,56,192]{2,1,0:T(8,128)} %get-tuple-element.290), calls=%async_computation.1 | async-start | bytes 458752 | tf_op jit(solution)/shard_map/all_to_all | solution.py:256
  17.8 0.0 copy-done.3
  17.8 1.1 %shard_map.64 = (s32[1]{0:T(128)}, s32[1]{0:T(128)}) custom-call(s32[2,128]{1,0:T(2,128)S(1)} %copy-done.3), custom_call_target="tpu_custom_call" | custom-call | tf_op jit(solution)/shard_map/pallas_call | solution.py:27
  19.5 18.1 %conditional.2 = (bf16[2,192,1280]{2,1,0:T(8,128)(2,1)}, bf16[2,192,1280]{2,1,0:T(8,128)(2,1)}, f32[16,192]{1,0:T(8,128)}, f32[16,192]{1,0:T(8,128)}) conditional(s32[]{:T(128)} %bitcast.1, (bf16[2,192,1280]{2,1,0:T(8,128)(2,1)S(1)}, f32[16,192]{1,0:T(8,128)S(1)}) %tuple.173, (bf16[2,192,1280]{2,1,0:T(8,128)(2,1)S(1)}, ...), branch_computations={%region_0.0_spmd, %region_1.0_spmd, %region_2.0_spmd, %region_3.0_... | conditional | bytes 7962816 | solution.py:270
  19.6 1.3 %collective-permute-start.21 = (bf16[2,192,1280]{2,1,0:T(8,128)(2,1)S(1)}, bf16[2,192,1280]{2,1,0:T(8,128)(2,1)}, u32[]{:S(2)}, u32[]{:S(2)}) collective-permute-start(bf16[2,192,1280]{2,1,0:T(8,128)(2,1)S(1)} %get-tuple-element.183), channel_id=1, source_target_pairs={{0,32},{2,34},{4,36},{6,38},{8,40},{10,42},{12,44},{14,46},{16,48}... | collective-permute-start | bytes 2949128 | tf_op jit(solution)/shard_map/cond/branch_5_fun/ppermute | solution.py:260
  20.9 1.3 %collective-permute-start.20 = (bf16[2,192,1280]{2,1,0:T(8,128)(2,1)S(1)}, bf16[2,192,1280]{2,1,0:T(8,128)(2,1)}, u32[]{:S(2)}, u32[]{:S(2)}) collective-permute-start(bf16[2,192,1280]{2,1,0:T(8,128)(2,1)S(1)} %get-tuple-element.183), channel_id=1, source_target_pairs={{0,16},{2,18},{4,20},{6,22},{8,24},{10,26},{12,28},{14,30},{17,1},... | collective-permute-start | bytes 2949128 | tf_op jit(solution)/shard_map/cond/branch_5_fun/ppermute | solution.py:260
  22.2 4.9 %collective-permute-start.23 = (f32[16,192]{1,0:T(8,128)S(1)}, f32[16,192]{1,0:T(8,128)}, u32[]{:S(2)}, u32[]{:S(2)}) collective-permute-start(f32[16,192]{1,0:T(8,128)S(1)} %get-tuple-element.184), channel_id=1, source_target_pairs={{0,32},{4,36},{8,40},{12,44},{16,48},{20,52},{24,56},{28,60},{32,0... | collective-permute-start | bytes 36872 | tf_op jit(solution)/shard_map/cond/branch_5_fun/ppermute | solution.py:261
  27.1 6.4 %collective-permute-start.22 = (f32[16,192]{1,0:T(8,128)S(1)}, f32[16,192]{1,0:T(8,128)}, u32[]{:S(2)}, u32[]{:S(2)}) collective-permute-start(f32[16,192]{1,0:T(8,128)S(1)} %get-tuple-element.184), channel_id=1, source_target_pairs={{0,16},{4,20},{8,24},{12,28},{16,0},{20,4},{24,8},{28,12},{32,48},... | collective-permute-start | bytes 36872 | tf_op jit(solution)/shard_map/cond/branch_5_fun/ppermute | solution.py:261
  33.6 1.4 %collective-permute-done.23 = f32[16,192]{1,0:T(8,128)} collective-permute-done((f32[16,192]{1,0:T(8,128)S(1)}, f32[16,192]{1,0:T(8,128)}, u32[]{:S(2)}, u32[]{:S(2)}) %collective-permute-start.23) | collective-permute-done | bytes 12320 | tf_op jit(solution)/shard_map/cond/branch_5_fun/ppermute | solution.py:261
  35.0 2.7 %collective-permute-done.22 = f32[16,192]{1,0:T(8,128)} collective-permute-done((f32[16,192]{1,0:T(8,128)S(1)}, f32[16,192]{1,0:T(8,128)}, u32[]{:S(2)}, u32[]{:S(2)}) %collective-permute-start.22) | collective-permute-done | bytes 12320 | tf_op jit(solution)/shard_map/cond/branch_5_fun/ppermute | solution.py:261
  37.7 0.0 collective-permute-done.21
  37.7 0.0 collective-permute-done.20
  37.7 3.6 %shard_map.66 = (f32[2,192,192]{2,1,0:T(8,128)S(1)}, f32[96,384]{1,0:T(8,128)S(1)}, f32[96,384]{1,0:T(8,128)S(1)}) custom-call(bf16[2,192,1280]{2,1,0:T(8,128)(2,1)} %get-tuple-element.279.first, bf16[2,192,1280]{2,1,0:T(8,128)(2,1)} %get-tuple-element.280.second, f32[8,1280]{1,0:T(8,128)S(1)} %get-tuple-element.281.rows, ...), custom_call_target="tpu_custom_call" | custom-call | tf_op jit(solution)/shard_map/pallas_call | solution.py:27
  41.3 9.1 %conditional.3 = (f32[96,384]{1,0:T(8,128)}, f32[96,384]{1,0:T(8,128)}) conditional(s32[]{:T(128)} %bitcast.1, (f32[96,384]{1,0:T(8,128)S(1)}, f32[96,384]{1,0:T(8,128)S(1)}) %tuple.174, (f32[96,384]{1,0:T(8,128)S(1)}, f32[96,384]{1,0:T(8,128)S(1)}) %tuple.174, (f32[96,384]{1,0:T(8,128)S(1)}, ...), branch_computations={%region_21.0_spmd, %region_22.0_spmd, %region_23.0_spmd, %region_2... | conditional | bytes 1179744 | solution.py:290
  41.3 3.2 %collective-permute-start.94 = (f32[96,384]{1,0:T(8,128)S(1)}, f32[96,384]{1,0:T(8,128)}, u32[]{:S(2)}, u32[]{:S(2)}) collective-permute-start(f32[96,384]{1,0:T(8,128)S(1)} %get-tuple-element.225), channel_id=1, source_target_pairs={{16,0},{18,2},{20,4},{22,6},{24,8},{26,10},{28,12},{30,14},{1,17},... | collective-permute-start | bytes 442376 | tf_op jit(solution)/shard_map/cond/branch_5_fun/ppermute | solution.py:266
  44.5 4.4 %collective-permute-start.95 = (f32[96,384]{1,0:T(8,128)S(1)}, f32[96,384]{1,0:T(8,128)}, u32[]{:S(2)}, u32[]{:S(2)}) collective-permute-start(f32[96,384]{1,0:T(8,128)S(1)} %get-tuple-element.226), channel_id=1, source_target_pairs={{32,0},{34,2},{36,4},{38,6},{40,8},{42,10},{44,12},{46,14},{48,16}... | collective-permute-start | bytes 442376 | tf_op jit(solution)/shard_map/cond/branch_5_fun/ppermute | solution.py:266
  48.9 0.0 collective-permute-done.94
  48.9 1.4 %collective-permute-done.95 = f32[96,384]{1,0:T(8,128)} collective-permute-done((f32[96,384]{1,0:T(8,128)S(1)}, f32[96,384]{1,0:T(8,128)}, u32[]{:S(2)}, u32[]{:S(2)}) %collective-permute-start.95) | collective-permute-done | bytes 147488 | tf_op jit(solution)/shard_map/cond/branch_5_fun/ppermute | solution.py:266
  50.4 1.9 %shard_map.67 = f32[4,56,384]{2,1,0:T(8,128)} custom-call(f32[2,192,192]{2,1,0:T(8,128)S(1)} %get-tuple-element.283.own, f32[96,384]{1,0:T(8,128)} %get-tuple-element.286.first, f32[96,384]{1,0:T(8,128)} %get-tuple-element.287.second, f32[16,192]{1,0:T(8,128)} %get-tuple-element.288.first_partial.refs_5_, f32[16,192]{1,0:T(8,128)} %get-tuple-element.289.second_partial.refs_6_), custom_call_target="tpu_custom_call" | custom-call | tf_op jit(solution)/shard_map/pallas_call | solution.py:27
  52.3 0.0 all-to-all-done.1.refs_1_
  52.3 4.5 %all-to-all-start = ((f32[4,56,384]{2,1,0:T(8,128)}), f32[4,56,384]{2,1,0:T(8,128)S(1)}, u32[]{:S(2)}, u32[]{:S(2)}) async-start(f32[4,56,384]{2,1,0:T(8,128)} %shard_map.67), calls=%async_computation | async-start | bytes 688128 | tf_op jit(solution)/shard_map/all_to_all | solution.py:300
  56.8 0.4 shard_map.68
  57.2 7.2 %all-to-all-done.refs_2_ = f32[4,56,384]{2,1,0:T(8,128)S(1)} async-done(((f32[4,56,384]{2,1,0:T(8,128)}), f32[4,56,384]{2,1,0:T(8,128)S(1)}, u32[]{:S(2)}, u32[]{:S(2)}) %all-to-all-start) | async-done | bytes 344096 | tf_op jit(solution)/shard_map/all_to_all | solution.py:300
  64.4 3.0 %shard_map.69 = f32[3,48,192]{2,1,0:T(8,128)} custom-call(s32[1]{0:T(128)} %get-tuple-element.275.refs_0_, s32[1]{0:T(128)} %bitcast.refs_0_.refs_1_, f32[4,56,384]{2,1,0:T(8,128)S(1)} %all-to-all-done.refs_2_, f32[8,192]{1,0:T(8,128)S(1)} %get-tuple-element.291.refs_3_, s32[1,192]{1,0:T(1,128)S(1)} %bitcast.6, ...), custom_call_target="tpu_custom_call" | custom-call | tf_op jit(solution)/shard_map/pallas_call | solution.py:27
  (1 shorter events, 0.0 us)
Async XLA Ops:
  0.0 0.7 %copy-start.4 = (s32[1280]{0:T(1024)S(1)}, s32[1280]{0:T(1024)}, u32[]{:S(2)}) copy-start(s32[1280]{0:T(1024)} %param.52) | copy-start | bytes 15364
  0.7 0.7 %copy-start.1 = (s32[192]{0:T(256)S(1)}, s32[192]{0:T(256)}, u32[]{:S(2)}) copy-start(s32[192]{0:T(256)} %param.49) | copy-start | bytes 2308
  0.7 0.7 copy-start.2
  1.4 1.2 %copy-start = (bf16[192,2,1280]{2,1,0:T(2,128)(2,1)S(1)}, bf16[192,2,1280]{2,1,0:T(2,128)(2,1)}, u32[]{:S(2)}) copy-start(bf16[192,2,1280]{2,1,0:T(2,128)(2,1)} %x.1) | copy-start | bytes 2949124
  7.4 10.4 %copy-start.3 = (s32[2,128]{1,0:T(2,128)S(1)}, s32[2,128]{1,0:T(2,128)}, u32[]{:S(2)}) copy-start(s32[2,128]{1,0:T(2,128)} %refs_0_.1) | copy-start | bytes 3076
  7.4 44.9 %all-to-all-start.1 = ((f32[4,56,192]{2,1,0:T(8,128)}), f32[4,56,192]{2,1,0:T(8,128)S(1)}, u32[]{:S(2)}, u32[]{:S(2)}) async-start(f32[4,56,192]{2,1,0:T(8,128)} %get-tuple-element.290), calls=%async_computation.1 | async-start | bytes 458752 | tf_op jit(solution)/shard_map/all_to_all | solution.py:256
  19.6 18.1 %collective-permute-start.21 = (bf16[2,192,1280]{2,1,0:T(8,128)(2,1)S(1)}, bf16[2,192,1280]{2,1,0:T(8,128)(2,1)}, u32[]{:S(2)}, u32[]{:S(2)}) collective-permute-start(bf16[2,192,1280]{2,1,0:T(8,128)(2,1)S(1)} %get-tuple-element.183), channel_id=1, source_target_pairs={{0,32},{2,34},{4,36},{6,38},{8,40},{10,42},{12,44},{14,46},{16,48}... | collective-permute-start | bytes 2949128 | tf_op jit(solution)/shard_map/cond/branch_5_fun/ppermute | solution.py:260
  20.9 16.8 %collective-permute-start.20 = (bf16[2,192,1280]{2,1,0:T(8,128)(2,1)S(1)}, bf16[2,192,1280]{2,1,0:T(8,128)(2,1)}, u32[]{:S(2)}, u32[]{:S(2)}) collective-permute-start(bf16[2,192,1280]{2,1,0:T(8,128)(2,1)S(1)} %get-tuple-element.183), channel_id=1, source_target_pairs={{0,16},{2,18},{4,20},{6,22},{8,24},{10,26},{12,28},{14,30},{17,1},... | collective-permute-start | bytes 2949128 | tf_op jit(solution)/shard_map/cond/branch_5_fun/ppermute | solution.py:260
  22.2 12.8 %collective-permute-start.23 = (f32[16,192]{1,0:T(8,128)S(1)}, f32[16,192]{1,0:T(8,128)}, u32[]{:S(2)}, u32[]{:S(2)}) collective-permute-start(f32[16,192]{1,0:T(8,128)S(1)} %get-tuple-element.184), channel_id=1, source_target_pairs={{0,32},{4,36},{8,40},{12,44},{16,48},{20,52},{24,56},{28,60},{32,0... | collective-permute-start | bytes 36872 | tf_op jit(solution)/shard_map/cond/branch_5_fun/ppermute | solution.py:261
  27.1 10.5 %collective-permute-start.22 = (f32[16,192]{1,0:T(8,128)S(1)}, f32[16,192]{1,0:T(8,128)}, u32[]{:S(2)}, u32[]{:S(2)}) collective-permute-start(f32[16,192]{1,0:T(8,128)S(1)} %get-tuple-element.184), channel_id=1, source_target_pairs={{0,16},{4,20},{8,24},{12,28},{16,0},{20,4},{24,8},{28,12},{32,48},... | collective-permute-start | bytes 36872 | tf_op jit(solution)/shard_map/cond/branch_5_fun/ppermute | solution.py:261
  41.3 7.6 %collective-permute-start.94 = (f32[96,384]{1,0:T(8,128)S(1)}, f32[96,384]{1,0:T(8,128)}, u32[]{:S(2)}, u32[]{:S(2)}) collective-permute-start(f32[96,384]{1,0:T(8,128)S(1)} %get-tuple-element.225), channel_id=1, source_target_pairs={{16,0},{18,2},{20,4},{22,6},{24,8},{26,10},{28,12},{30,14},{1,17},... | collective-permute-start | bytes 442376 | tf_op jit(solution)/shard_map/cond/branch_5_fun/ppermute | solution.py:266
  44.5 5.9 %collective-permute-start.95 = (f32[96,384]{1,0:T(8,128)S(1)}, f32[96,384]{1,0:T(8,128)}, u32[]{:S(2)}, u32[]{:S(2)}) collective-permute-start(f32[96,384]{1,0:T(8,128)S(1)} %get-tuple-element.226), channel_id=1, source_target_pairs={{32,0},{34,2},{36,4},{38,6},{40,8},{42,10},{44,12},{46,14},{48,16}... | collective-permute-start | bytes 442376 | tf_op jit(solution)/shard_map/cond/branch_5_fun/ppermute | solution.py:266
  52.3 12.1 %all-to-all-start = ((f32[4,56,384]{2,1,0:T(8,128)}), f32[4,56,384]{2,1,0:T(8,128)S(1)}, u32[]{:S(2)}, u32[]{:S(2)}) async-start(f32[4,56,384]{2,1,0:T(8,128)} %shard_map.67), calls=%async_computation | async-start | bytes 688128 | tf_op jit(solution)/shard_map/all_to_all | solution.py:300

commit v2 on v1

v2 whole, which is shorter than its diff:
```python
import math

import jax
import jax.numpy as jnp
from jax import lax
from jax.experimental import pallas as pl
from jax.experimental.pallas import tpu as pltpu
from jax.sharding import PartitionSpec as P

first_shell = 4
first_limit = 48
limit_step = 3
class_count = 8
epsilon = 1e-05
front_vmem = 60 << 20

f32 = jnp.float32
bf16 = jnp.bfloat16
in_vmem = pl.BlockSpec(memory_space=pltpu.VMEM)
in_hbm = pl.BlockSpec(memory_space=pltpu.HBM)
in_smem = pl.BlockSpec(memory_space=pltpu.SMEM)


def shape(dims, dtype):
    return jax.ShapeDtypeStruct(dims, dtype)


def local_call(kernel, out_shape, in_specs, out_specs, args, scratch=(), vmem=40 << 20):
    return pl.pallas_call(
        kernel,
        out_shape=out_shape,
        in_specs=in_specs,
        out_specs=out_specs,
        scratch_shapes=scratch,
        compiler_params=pltpu.CompilerParams(vmem_limit_bytes=vmem),
    )(*args)


def contract(left_side, right_side):
    return lax.dot_general(
        left_side, right_side, (((1,), (1,)), ((), ())), preferred_element_type=f32
    )


def one_way(blocks, voxes, bit):
    return [
        (b * voxes + v, (b ^ 1 << bit) * voxes + v)
        for b in range(blocks)
        for v in range(voxes)
        if v & 1 == b >> bit & 1
    ]


def back(pairs):
    return [(target, source) for source, target in pairs]


def both_ways(blocks, bit):
    return [(b, b ^ 1 << bit) for b in range(blocks)]


def column(row):
    return jnp.broadcast_to(row, (8, row.shape[1])).T[:, 0:1]


def limits_of(labels):
    return first_limit + 1.0 + limit_step * column(labels.astype(f32))


def chunk_of(width):
    return next(size for size in (256, 128, width) if width % size == 0)


def mask_kernel(
    bit_count, x, labels, plan, shells, angles, gain, index_out, flag_out, left_out, *scratch
):
    rows, buffers, sems = scratch[0], scratch[1:-1], scratch[-1]
    half = left_out.shape[1] // 2
    block, labels_in, plan_in, shells_in, angles_in, gain_in = buffers
    halves = [
        pltpu.make_async_copy(
            x.at[pl.ds(half * h, half)], block.at[pl.ds(half * h, half)], sems.at[h]
        )
        for h in range(2)
    ]
    small = [
        pltpu.make_async_copy(source, buffer, sems.at[2 + i])
        for i, (source, buffer) in enumerate(
            zip((labels, plan, shells, angles, gain), buffers[1:])
        )
    ]
    for copy in small + halves:
        copy.start()
    for copy in small:
        copy.wait()

    def bit_of(value):
        return sum([jnp.where(value >= 1 << k, 1, 0) for k in range(1, bit_count)])

    first, second = bit_of(plan_in[0, 0]), bit_of(plan_in[1, 0])
    low, high = jnp.minimum(first, second), jnp.maximum(first, second)
    index_out[0] = high * (high - 1) // 2 + low
    flag_out[0] = jnp.where(first > second, 1, 0)

    shell_row = shells_in[...].reshape(1, -1)
    angle_row = angles_in[...].reshape(1, -1).astype(f32)
    weights = jnp.zeros(shell_row.shape, f32)
    for s in range(gain.shape[0]):
        weights = jnp.where(shell_row == s + first_shell, gain_in[s], weights)
    rows[0:1, :] = weights.astype(bf16).astype(f32)
    rows[1:2, :] = angle_row
    limits = limits_of(labels_in[...].reshape(1, -1)).astype(bf16)
    chunk = chunk_of(x.shape[2])
    for h in range(2):
        halves[h].wait()

        def step(i, carry):
            at = pl.ds(pl.multiple_of(i * chunk, chunk), chunk)
            keep = jnp.clip(
                limits[half * h : half * (h + 1)] - rows[1:2, at].astype(bf16), 0, 1
            )
            parts = jnp.swapaxes(block[half * h : half * (h + 1), :, at], 0, 1)
            for t in range(2):
                left_out[t, half * h : half * (h + 1), at] = parts[t] * keep
            return carry

        lax.fori_loop(0, x.shape[2] // chunk, step, 0)


def own_kernel(left, rows, labels, message, partial, acc, sums):
    chunk = chunk_of(left.shape[2])
    limits = first_limit + limit_step * lax.broadcasted_iota(jnp.int32, (class_count, 1), 0)
    limits = limits.astype(f32)
    acc[...] = jnp.zeros(acc.shape, f32)
    sums[...] = jnp.zeros(sums.shape, f32)

    def step(i, carry):
        at = pl.ds(pl.multiple_of(i * chunk, chunk), chunk)
        weights = rows[0:1, at].astype(bf16)
        table = jnp.where(rows[1:2, at] <= limits, rows[0:1, at], 0.0).astype(bf16)
        parts = [left[t, :, at] for t in range(2)]
        wide = [part.astype(f32) for part in parts]
        power = (wide[0] * wide[0] + wide[1] * wide[1]).astype(bf16)
        sums[...] += contract(table, power)
        acc[...] += contract(parts[0] * weights, parts[0]) + contract(parts[1] * weights, parts[1])
        return carry

    lax.fori_loop(0, left.shape[2] // chunk, step, 0)
    parts, height = message.shape[0], message.shape[1] - class_count
    for q in range(parts):
        message[q, 0:height, :] = acc[height * q : height * (q + 1), :]
        message[q, height:, :] = sums[...]
    partial[0:class_count, :] = sums[...]
    partial[class_count:, :] = jnp.broadcast_to(labels[...].astype(f32), sums.shape)


def norms(own_sums, own_labels, slice_sums, slice_labels, total):
    left_norm = jnp.zeros((slice_sums.shape[0], own_sums.shape[1]), f32)
    right_norm = left_norm
    for c in range(class_count):
        left_norm = jnp.where(slice_labels == c, own_sums[c : c + 1, :], left_norm)
        right_norm = jnp.where(own_labels == c, slice_sums[:, c : c + 1], right_norm)
    return lax.rsqrt((left_norm / total + epsilon) * (right_norm / total + epsilon)) / math.sqrt(
        total
    )


def sliced(place, height, sums, labels, scratch):
    scratch[:, 0:class_count] = sums.T
    scratch[:, class_count : 2 * class_count] = jnp.broadcast_to(
        labels, (class_count, labels.shape[1])
    ).T
    part = scratch[pl.ds(pl.multiple_of(place[0] * height, 8), height), :]
    return part[:, 0:class_count], part[:, class_count : class_count + 1]


def summed_of(message):
    summed = message[0]
    for q in range(1, message.shape[0]):
        summed = summed + message[q]
    return summed


def self_kernel(total, place, message, labels, sums_out, out, scratch):
    height = message.shape[1] - class_count
    summed = summed_of(message)
    sums = summed[height:, :]
    own_labels = labels[...].astype(f32)
    sums_out[...] = sums
    slice_sums, slice_labels = sliced(place, height, sums, own_labels, scratch)
    out[...] = summed[0:height, :] * norms(sums, own_labels, slice_sums, slice_labels, total)


def pair_kernel(first, second, rows, left, own_out, first_out, second_out, blocks, sems):
    count = own_out.shape[2]
    copies = [
        [
            pltpu.make_async_copy(
                block.at[t], blocks.at[t, pl.ds(count * s, count)], sems.at[2 * t + s]
            )
            for s, block in enumerate((first, second))
        ]
        for t in range(2)
    ]
    for pair in copies:
        for copy in pair:
            copy.start()
    weights = rows[0:1, :].astype(bf16)
    own_sum, sent_sum = None, None
    for t in range(2):
        for copy in copies[t]:
            copy.wait()
        other, own = blocks[t], left[t]
        own_part, sent_part = contract(other * weights, own), contract(other, own * weights)
        own_sum = own_part if own_sum is None else own_sum + own_part
        sent_sum = sent_part if sent_sum is None else sent_sum + sent_part
    half = first_out.shape[0]
    for s, out in enumerate((first_out, second_out)):
        own_out[s] = own_sum[count * s : count * (s + 1)]
        sent = sent_sum[count * s : count * (s + 1)].T
        out[:, 0:count] = sent[0:half]
        out[:, count:] = sent[half:]


def merge_kernel(own, first, second, first_partial, second_partial, out):
    parts, height = out.shape[0], out.shape[1] - class_count
    count = own.shape[2]
    for s, (received, partial) in enumerate(((first, first_partial), (second, second_partial))):
        half = received.shape[0]
        across = slice(count * s, count * (s + 1))
        for q in range(parts):
            side, at = divmod(q * height, half)
            out[q, 0:height, across] = (
                own[s, height * q : height * (q + 1), :]
                + received[at : at + height, count * side : count * (side + 1)]
            )
            out[q, height:, across] = partial[0:class_count, :]


def last_kernel(
    total, flag, place, pieces, sums, labels, first_partial, second_partial, self_out, out, scratch
):
    count, height = out.shape[2], out.shape[1]
    summed = summed_of(pieces)
    own_labels = labels[...].astype(f32)
    out[0] = self_out[...]
    for s, partial in enumerate((first_partial, second_partial)):
        mine = summed[:, count * s : count * (s + 1)]
        slice_sums, slice_labels = sliced(
            place, height, mine[height:, :], partial[class_count : class_count + 1, :], scratch
        )
        out[1 + (s ^ flag[0])] = mine[0:height, :] * norms(
            sums[...], own_labels, slice_sums, slice_labels, total
        )


def body(particles, classes, plan, voxel_shell, voxel_angle, shell_gain):
    blocks, voxes = lax.axis_size("blk"), lax.axis_size("vox")
    bit_count = blocks.bit_length() - 1
    count, _, width = particles.shape
    height, total = count // voxes, width * voxes
    axes = ("blk", "vox")
    bit_pairs = [(low, high) for high in range(bit_count) for low in range(high)]

    def mask_call(*refs):
        mask_kernel(bit_count, *refs)

    def self_call(*refs):
        self_kernel(total, *refs)

    def last_call(*refs):
        last_kernel(total, *refs)

    place = lax.axis_index("vox").reshape(1)
    labels = classes.reshape(1, -1)
    arrays = (particles, classes, plan, voxel_shell, voxel_angle, shell_gain)
    spaces = (pltpu.VMEM, pltpu.VMEM, pltpu.SMEM, pltpu.VMEM, pltpu.VMEM, pltpu.SMEM)
    index, flag, left, rows = local_call(
        mask_call,
        (
            shape((1,), jnp.int32),
            shape((1,), jnp.int32),
            shape((2, count, width), bf16),
            shape((8, width), f32),
        ),
        [in_hbm] * len(arrays),
        (in_smem, in_smem, in_vmem, in_vmem),
        arrays,
        [space(array.shape, array.dtype) for space, array in zip(spaces, arrays)]
        + [pltpu.SemaphoreType.DMA((1 + len(arrays),))],
        front_vmem,
    )
    index = index[0]
    scratch = [pltpu.VMEM((count, 2 * class_count), f32)]

    def fetch(bits):
        pairs = [one_way(blocks, voxes, bit) for bit in bits]

        def run(left, rows, labels, place):
            blocks_in = [lax.ppermute(left, axes, pair) for pair in pairs]
            message, partial = local_call(
                own_kernel,
                (
                    shape((voxes, height + class_count, count), f32),
                    shape((2 * class_count, count), f32),
                ),
                [in_vmem] * 3,
                (in_vmem, in_vmem),
                (left, rows, labels),
                [pltpu.VMEM((count, count), f32), pltpu.VMEM((class_count, count), f32)],
            )
            partials_in = [lax.ppermute(partial, "blk", both_ways(blocks, bit)) for bit in bits]
            message = lax.all_to_all(message, "vox", 0, 0, tiled=True)
            sums, self_out = local_call(
                self_call,
                (shape((class_count, count), f32), shape((height, count), f32)),
                [in_smem, in_vmem, in_vmem],
                (in_vmem, in_vmem),
                (place, message, labels),
                scratch,
            )
            return (*blocks_in, *partials_in, sums, self_out)

        return run

    def give_back(bits):
        return lambda *sent: tuple(
            lax.ppermute(part, axes, back(one_way(blocks, voxes, bit)))
            for part, bit in zip(sent, bits)
        )

    first, second, first_partial, second_partial, sums, self_out = lax.switch(
        index, [fetch(bits) for bits in bit_pairs], left, rows, labels, place
    )
    own, first_sent, second_sent = local_call(
        pair_kernel,
        (shape((2, count, count), f32),) + (shape((count // 2, 2 * count), f32),) * 2,
        [in_hbm, in_hbm, in_vmem, in_vmem],
        (in_vmem,) * 3,
        (first, second, rows, left),
        [pltpu.VMEM((2, 2 * count, width), bf16), pltpu.SemaphoreType.DMA((4,))],
    )
    first_back, second_back = lax.switch(
        index, [give_back(bits) for bits in bit_pairs], first_sent, second_sent
    )
    merged = local_call(
        merge_kernel,
        shape((voxes, height + class_count, 2 * count), f32),
        [in_vmem] * 5,
        in_vmem,
        (own, first_back, second_back, first_partial, second_partial),
    )
    pieces = lax.all_to_all(merged, "vox", 0, 0, tiled=True)
    out = local_call(
        last_call,
        shape((3, height, count), f32),
        [in_smem, in_smem] + [in_vmem] * 6,
        in_vmem,
        (flag, place, pieces, sums, labels, first_partial, second_partial, self_out),
        scratch,
    )
    return out.transpose(0, 2, 1)


def solution(mesh):
    in_specs = (P("blk", None, "vox"), P("blk"), P(), P("vox"), P("vox"), P())
    out_specs = P(None, "blk", "vox")
    return jax.shard_map(body, mesh=mesh, in_specs=in_specs, out_specs=out_specs, check_vma=False)
```

time: 68 us -> 110 us (1.62)
  the two profiles are of different devices: /device:TPU:1 before, /device:TPU:24 now
where the time goes in v2:
time: 110 us
  waiting for transfers between devices  41.7 us (38%)
  starting transfers between devices  41.2 us (37%)
  blocking collectives  12.5 us (11%)
  Pallas kernels  12.3 us (11%)
    ppermute x2, waiting for transfers between devices, run(): lax.ppermute(partial, 'blk', both_ways(blocks, bit))  27.1 us
    ppermute x2, starting transfers between devices, run(): blocks_in = [lax.ppermute(left, axes, pair) for pair in pairs]  18 us
    ppermute x2, waiting for transfers between devices, give_back(): lax.ppermute(part, axes, back(one_way(blocks, voxes, bit)))  14.6 us
    all_to_all x1, blocking collectives, body(): pieces = lax.all_to_all(merged, 'vox', 0, 0, tiled=True)  12.5 us
    pallas_call x6, Pallas kernels, local_call(): pl.pallas_call(kernel, out_shape=out_shape, in_specs=in_specs, out_specs=...  12.3 us
    ppermute x2, starting transfers between devices, give_back(): lax.ppermute(part, axes, back(one_way(blocks, voxes, bit)))  9.96 us
    ppermute x2, starting transfers between devices, run(): lax.ppermute(partial, 'blk', both_ways(blocks, bit))  8.93 us
    all_to_all x1, starting transfers between devices, run(): message = lax.all_to_all(message, 'vox', 0, 0, tiled=True)  4.3 us
  transfers between devices with their start and end apart: 7, of which 3 were waited for; matrix products, arithmetic and copies ran while one was open for 0% of the time, Pallas kernels for 2%

profile of v2, /device:TPU:24, one launch (start us, length us, event | category | flops | bytes accessed | tf_op | source)
XLA Modules:
  0.0 109.6 jit_solution(12493338852660107892)
XLA Ops:
  0.0 0.0 copy-start
  0.0 0.7 copy-done
  0.7 2.8 %shard_map.64 = (s32[1]{0:T(128)}, s32[1]{0:T(128)}, bf16[2,192,1280]{2,1,0:T(8,128)(2,1)S(1)}, f32[8,1280]{1,0:T(8,128)S(1)}) custom-call(bf16[192,2,1280]{2,1,0:T(2,128)(2,1)} %refs_0_.1, s32[192]{0:T(256)S(1)} %copy-done, s32[2,128]{1,0:T(2,128)} %refs_2_.1, s32[1280]{0:T(1024)} %refs_3_.1, s32[1280]{0:T(1024)} %refs_4_.1, f32[13]{0:T(128)} %refs_5_.1), custom_call_target="tpu_custom_call" | custom-call | tf_op jit(solution)/shard_map/pallas_call | solution.py:29
  4.1 61.3 %conditional.2 = (bf16[2,192,1280]{2,1,0:T(8,128)(2,1)}, bf16[2,192,1280]{2,1,0:T(8,128)(2,1)}, f32[16,192]{1,0:T(8,128)}, f32[16,192]{1,0:T(8,128)}, f32[8,192]{1,0:T(8,128)S(1)}, /*index=5*/f32[48,192]{1,0:T(8,128)S(1)}) conditional(s32[]{:T(128)} %bitcast.1, (bf16[2,192,1280]{2,1,0:T(8,128)(2,1)S(1)}, ...), branch_computations={%region_0.0_spmd, %region_1.0_spmd, %region_2.0_spmd, %region_3.0_... | conditional | bytes 8593648 | solution.py:332
  4.4 16.7 %collective-permute-start.69 = (bf16[2,192,1280]{2,1,0:T(8,128)(2,1)S(1)}, bf16[2,192,1280]{2,1,0:T(8,128)(2,1)}, u32[]{:S(2)}, u32[]{:S(2)}) collective-permute-start(bf16[2,192,1280]{2,1,0:T(8,128)(2,1)S(1)} %get-tuple-element.393.left), channel_id=1, source_target_pairs={{0,256},{2,258},{4,260},{6,262},{8,264},{10,266},{12,268},{14,270}... | collective-permute-start | bytes 2949128 | tf_op jit(solution)/shard_map/cond/branch_17_fun/ppermute | solution.py:300
  21.1 1.3 %collective-permute-start.68 = (bf16[2,192,1280]{2,1,0:T(8,128)(2,1)S(1)}, bf16[2,192,1280]{2,1,0:T(8,128)(2,1)}, u32[]{:S(2)}, u32[]{:S(2)}) collective-permute-start(bf16[2,192,1280]{2,1,0:T(8,128)(2,1)S(1)} %get-tuple-element.393.left), channel_id=1, source_target_pairs={{0,16},{2,18},{4,20},{6,22},{8,24},{10,26},{12,28},{14,30},{17,1},... | collective-permute-start | bytes 2949128 | tf_op jit(solution)/shard_map/cond/branch_17_fun/ppermute | solution.py:300
  22.4 2.0 %branch_17_fun.2 = (f32[4,56,192]{2,1,0:T(8,128)}, f32[16,192]{1,0:T(8,128)S(1)}) custom-call(bf16[2,192,1280]{2,1,0:T(8,128)(2,1)S(1)} %get-tuple-element.393.left, f32[8,1280]{1,0:T(8,128)S(1)} %get-tuple-element.394.rows, s32[1,192]{1,0:T(1,128)S(1)} %get-tuple-element.395.labels.refs_2_), custom_call_target="tpu_custom_call" | custom-call | tf_op jit(solution)/shard_map/cond/branch_17_fun/pallas_call | solution.py:29
  24.4 4.3 %all-to-all-start.17 = ((f32[4,56,192]{2,1,0:T(8,128)}), f32[4,56,192]{2,1,0:T(8,128)S(1)}, u32[]{:S(2)}, u32[]{:S(2)}) async-start(f32[4,56,192]{2,1,0:T(8,128)} %get-tuple-element.398), calls=%async_computation.17 | async-start | bytes 458752 | tf_op jit(solution)/shard_map/cond/branch_17_fun/all_to_all | solution.py:313
  28.7 3.3 %collective-permute-start.71 = (f32[16,192]{1,0:T(8,128)S(1)}, f32[16,192]{1,0:T(8,128)}, u32[]{:S(2)}, u32[]{:S(2)}) collective-permute-start(f32[16,192]{1,0:T(8,128)S(1)} %get-tuple-element.396), channel_id=1, source_target_pairs={{0,256},{4,260},{8,264},{12,268},{16,272},{20,276},{24,280},{28,28... | collective-permute-start | bytes 36872 | tf_op jit(solution)/shard_map/cond/branch_17_fun/ppermute | solution.py:312
  32.0 5.7 %collective-permute-start.70 = (f32[16,192]{1,0:T(8,128)S(1)}, f32[16,192]{1,0:T(8,128)}, u32[]{:S(2)}, u32[]{:S(2)}) collective-permute-start(f32[16,192]{1,0:T(8,128)S(1)} %get-tuple-element.396), channel_id=1, source_target_pairs={{0,16},{4,20},{8,24},{12,28},{16,0},{20,4},{24,8},{28,12},{32,48},... | collective-permute-start | bytes 36872 | tf_op jit(solution)/shard_map/cond/branch_17_fun/ppermute | solution.py:312
  37.6 0.0 all-to-all-done.17.refs_1_
  37.7 0.4 branch_17_fun.3
  38.1 27.1 %collective-permute-done.71 = f32[16,192]{1,0:T(8,128)} collective-permute-done((f32[16,192]{1,0:T(8,128)S(1)}, f32[16,192]{1,0:T(8,128)}, u32[]{:S(2)}, u32[]{:S(2)}) %collective-permute-start.71) | collective-permute-done | bytes 12320 | tf_op jit(solution)/shard_map/cond/branch_17_fun/ppermute | solution.py:312
  65.2 0.0 collective-permute-done.70
  65.2 0.0 collective-permute-done.69
  65.2 0.0 collective-permute-done.68
  65.4 2.9 %shard_map.65 = (f32[2,192,192]{2,1,0:T(8,128)S(1)}, f32[96,384]{1,0:T(8,128)S(1)}, f32[96,384]{1,0:T(8,128)S(1)}) custom-call(bf16[2,192,1280]{2,1,0:T(8,128)(2,1)} %get-tuple-element.486.first, bf16[2,192,1280]{2,1,0:T(8,128)(2,1)} %get-tuple-element.487.second, f32[8,1280]{1,0:T(8,128)S(1)} %get-tuple-element.485.rows, ...), custom_call_target="tpu_custom_call" | custom-call | tf_op jit(solution)/shard_map/pallas_call | solution.py:29
  68.4 24.6 %conditional.3 = (f32[96,384]{1,0:T(8,128)}, f32[96,384]{1,0:T(8,128)}) conditional(s32[]{:T(128)} %bitcast.1, (f32[96,384]{1,0:T(8,128)S(1)}, f32[96,384]{1,0:T(8,128)S(1)}) %tuple.174, (f32[96,384]{1,0:T(8,128)S(1)}, f32[96,384]{1,0:T(8,128)S(1)}) %tuple.174, (f32[96,384]{1,0:T(8,128)S(1)}, ...), branch_computations={%region_21.0_spmd, %region_22.0_spmd, %region_23.0_spmd, %region_2... | conditional | bytes 1179744 | solution.py:343
  68.4 8.7 %collective-permute-start.118 = (f32[96,384]{1,0:T(8,128)S(1)}, f32[96,384]{1,0:T(8,128)}, u32[]{:S(2)}, u32[]{:S(2)}) collective-permute-start(f32[96,384]{1,0:T(8,128)S(1)} %get-tuple-element.459), channel_id=1, source_target_pairs={{16,0},{18,2},{20,4},{22,6},{24,8},{26,10},{28,12},{30,14},{1,17},... | collective-permute-start | bytes 442376 | tf_op jit(solution)/shard_map/cond/branch_17_fun/ppermute | solution.py:328
  77.1 1.3 %collective-permute-start.119 = (f32[96,384]{1,0:T(8,128)S(1)}, f32[96,384]{1,0:T(8,128)}, u32[]{:S(2)}, u32[]{:S(2)}) collective-permute-start(f32[96,384]{1,0:T(8,128)S(1)} %get-tuple-element.460), channel_id=1, source_target_pairs={{256,0},{258,2},{260,4},{262,6},{264,8},{266,10},{268,12},{270,14}... | collective-permute-start | bytes 442376 | tf_op jit(solution)/shard_map/cond/branch_17_fun/ppermute | solution.py:328
  78.4 0.7 collective-permute-done.118
  79.1 13.8 %collective-permute-done.119 = f32[96,384]{1,0:T(8,128)} collective-permute-done((f32[96,384]{1,0:T(8,128)S(1)}, f32[96,384]{1,0:T(8,128)}, u32[]{:S(2)}, u32[]{:S(2)}) %collective-permute-start.119) | collective-permute-done | bytes 147488 | tf_op jit(solution)/shard_map/cond/branch_17_fun/ppermute | solution.py:328
  92.9 1.2 %shard_map.66 = f32[4,56,384]{2,1,0:T(8,128)S(1)} custom-call(f32[2,192,192]{2,1,0:T(8,128)S(1)} %get-tuple-element.488.own, f32[96,384]{1,0:T(8,128)} %get-tuple-element.491.first, f32[96,384]{1,0:T(8,128)} %get-tuple-element.492.second, f32[16,192]{1,0:T(8,128)} %get-tuple-element.493.first_partial.refs_5_, f32[16,192]{1,0:T(8,128)} %get-tuple-element.494.second_partial.refs_6_), custom_call_target="tpu_custom_call" | custom-call | tf_op jit(solution)/shard_map/pallas_call | solution.py:29
  94.1 12.5 %all_to_all.89.refs_2_ = f32[4,56,384]{2,1,0:T(8,128)S(1)} all-to-all(f32[4,56,384]{2,1,0:T(8,128)S(1)} %shard_map.66), channel_id=1, replica_groups=mesh['blk'=128,'vox'=4] {'vox'}, dimensions={0} | all-to-all | bytes 688128 | tf_op jit(solution)/shard_map/all_to_all | solution.py:353
  106.7 3.0 %shard_map.67 = f32[3,48,192]{2,1,0:T(8,128)} custom-call(s32[1]{0:T(128)} %get-tuple-element.482.refs_0_, s32[1]{0:T(128)} %bitcast.refs_1_, f32[4,56,384]{2,1,0:T(8,128)S(1)} %all_to_all.89.refs_2_, f32[8,192]{1,0:T(8,128)S(1)} %get-tuple-element.495.refs_3_, s32[1,192]{1,0:T(1,128)S(1)} %bitcast.25, f32[16,192]{1,0:T(8,128)} %get-tuple-element.493.first_partial.refs_5_, ...), custom_call_target="tpu_custom_call" | custom-call | tf_op jit(solution)/shard_map/pallas_call | solution.py:29
Async XLA Ops:
  0.0 0.7 copy-start
  4.4 60.8 %collective-permute-start.69 = (bf16[2,192,1280]{2,1,0:T(8,128)(2,1)S(1)}, bf16[2,192,1280]{2,1,0:T(8,128)(2,1)}, u32[]{:S(2)}, u32[]{:S(2)}) collective-permute-start(bf16[2,192,1280]{2,1,0:T(8,128)(2,1)S(1)} %get-tuple-element.393.left), channel_id=1, source_target_pairs={{0,256},{2,258},{4,260},{6,262},{8,264},{10,266},{12,268},{14,270}... | collective-permute-start | bytes 2949128 | tf_op jit(solution)/shard_map/cond/branch_17_fun/ppermute | solution.py:300
  21.1 44.1 %collective-permute-start.68 = (bf16[2,192,1280]{2,1,0:T(8,128)(2,1)S(1)}, bf16[2,192,1280]{2,1,0:T(8,128)(2,1)}, u32[]{:S(2)}, u32[]{:S(2)}) collective-permute-start(bf16[2,192,1280]{2,1,0:T(8,128)(2,1)S(1)} %get-tuple-element.393.left), channel_id=1, source_target_pairs={{0,16},{2,18},{4,20},{6,22},{8,24},{10,26},{12,28},{14,30},{17,1},... | collective-permute-start | bytes 2949128 | tf_op jit(solution)/shard_map/cond/branch_17_fun/ppermute | solution.py:300
  24.4 13.3 %all-to-all-start.17 = ((f32[4,56,192]{2,1,0:T(8,128)}), f32[4,56,192]{2,1,0:T(8,128)S(1)}, u32[]{:S(2)}, u32[]{:S(2)}) async-start(f32[4,56,192]{2,1,0:T(8,128)} %get-tuple-element.398), calls=%async_computation.17 | async-start | bytes 458752 | tf_op jit(solution)/shard_map/cond/branch_17_fun/all_to_all | solution.py:313
  28.7 36.5 %collective-permute-start.71 = (f32[16,192]{1,0:T(8,128)S(1)}, f32[16,192]{1,0:T(8,128)}, u32[]{:S(2)}, u32[]{:S(2)}) collective-permute-start(f32[16,192]{1,0:T(8,128)S(1)} %get-tuple-element.396), channel_id=1, source_target_pairs={{0,256},{4,260},{8,264},{12,268},{16,272},{20,276},{24,280},{28,28... | collective-permute-start | bytes 36872 | tf_op jit(solution)/shard_map/cond/branch_17_fun/ppermute | solution.py:312
  32.0 33.2 %collective-permute-start.70 = (f32[16,192]{1,0:T(8,128)S(1)}, f32[16,192]{1,0:T(8,128)}, u32[]{:S(2)}, u32[]{:S(2)}) collective-permute-start(f32[16,192]{1,0:T(8,128)S(1)} %get-tuple-element.396), channel_id=1, source_target_pairs={{0,16},{4,20},{8,24},{12,28},{16,0},{20,4},{24,8},{28,12},{32,48},... | collective-permute-start | bytes 36872 | tf_op jit(solution)/shard_map/cond/branch_17_fun/ppermute | solution.py:312
  68.4 10.7 %collective-permute-start.118 = (f32[96,384]{1,0:T(8,128)S(1)}, f32[96,384]{1,0:T(8,128)}, u32[]{:S(2)}, u32[]{:S(2)}) collective-permute-start(f32[96,384]{1,0:T(8,128)S(1)} %get-tuple-element.459), channel_id=1, source_target_pairs={{16,0},{18,2},{20,4},{22,6},{24,8},{26,10},{28,12},{30,14},{1,17},... | collective-permute-start | bytes 442376 | tf_op jit(solution)/shard_map/cond/branch_17_fun/ppermute | solution.py:328
  77.1 15.8 %collective-permute-start.119 = (f32[96,384]{1,0:T(8,128)S(1)}, f32[96,384]{1,0:T(8,128)}, u32[]{:S(2)}, u32[]{:S(2)}) collective-permute-start(f32[96,384]{1,0:T(8,128)S(1)} %get-tuple-element.460), channel_id=1, source_target_pairs={{256,0},{258,2},{260,4},{262,6},{264,8},{266,10},{268,12},{270,14}... | collective-permute-start | bytes 442376 | tf_op jit(solution)/shard_map/cond/branch_17_fun/ppermute | solution.py:328

commit v3 on v2

--- a/solution.py
+++ b/solution.py
@@ -49,6 +49,15 @@
         for v in range(voxes)
         if v & 1 == b >> bit & 1
     ]
+
+
+def both_cores(blocks, voxes, bit):
+    return [(b * voxes + v, (b ^ 1 << bit) * voxes + v) for b in range(blocks) for v in range(voxes)]
+
+
+def sent_whole(bits):
+    axis = [0 if bit == 0 else 1 if bit < 3 else 2 for bit in bits]
+    return tuple(axis[0] != axis[1] and bit < 4 and bits[1] != 4 for bit in bits)
 
 
 def back(pairs):
@@ -222,35 +231,53 @@
         out[:, count:] = sent[half:]
 
 
-def merge_kernel(own, first, second, first_partial, second_partial, out):
+def merge_kernel(whole, own, first_partial, second_partial, *refs):
+    received, out = list(refs[:-1]), refs[-1]
     parts, height = out.shape[0], out.shape[1] - class_count
     count = own.shape[2]
-    for s, (received, partial) in enumerate(((first, first_partial), (second, second_partial))):
-        half = received.shape[0]
+    for s, partial in enumerate((first_partial, second_partial)):
+        back_in = None if whole[s] else received.pop(0)
         across = slice(count * s, count * (s + 1))
         for q in range(parts):
-            side, at = divmod(q * height, half)
-            out[q, 0:height, across] = (
-                own[s, height * q : height * (q + 1), :]
-                + received[at : at + height, count * side : count * (side + 1)]
-            )
+            scores = own[s, height * q : height * (q + 1), :]
+            if back_in is not None:
+                side, at = divmod(q * height, back_in.shape[0])
+                scores += back_in[at : at + height, count * side : count * (side + 1)]
+            out[q, 0:height, across] = scores
             out[q, height:, across] = partial[0:class_count, :]
 
 
-def last_kernel(
-    total, flag, place, pieces, sums, labels, first_partial, second_partial, self_out, out, scratch
-):
+def left_kernel(total, place, sums, labels, first_partial, second_partial, self_out, out, scratch):
+    count, height = out.shape[2], out.shape[1]
+    out[0] = self_out[...]
+    for s, partial in enumerate((first_partial, second_partial)):
+        scratch[...] = partial[class_count:, :].T
+        part = scratch[pl.ds(pl.multiple_of(place[0] * height, 8), height), 0:1]
+        norm = jnp.zeros((height, count), f32)
+        for c in range(class_count):
+            norm = jnp.where(part == c, sums[c : c + 1, :], norm)
+        out[1 + s] = lax.rsqrt(norm / total + epsilon) / math.sqrt(total)
+
+
+def last_kernel(total, flag, place, pieces, factors, labels, out, scratch):
     count, height = out.shape[2], out.shape[1]
     summed = summed_of(pieces)
-    own_labels = labels[...].astype(f32)
-    out[0] = self_out[...]
-    for s, partial in enumerate((first_partial, second_partial)):
-        mine = summed[:, count * s : count * (s + 1)]
-        slice_sums, slice_labels = sliced(
-            place, height, mine[height:, :], partial[class_count : class_count + 1, :], scratch
-        )
-        out[1 + (s ^ flag[0])] = mine[0:height, :] * norms(
-            sums[...], own_labels, slice_sums, slice_labels, total
+    own_labels = labels[...]
+    out[0] = factors[0]
+    for s in range(2):
+        scratch[:, class_count * s : class_count * (s + 1)] = summed[
+            height:, count * s : count * (s + 1)
+        ].T
+    part = scratch[pl.ds(pl.multiple_of(place[0] * height, 8), height), :]
+    for s in range(2):
+        norm = jnp.zeros((height, count), f32)
+        for c in range(class_count):
+            at = class_count * s + c
+            norm = jnp.where(own_labels == c, part[:, at : at + 1], norm)
+        out[1 + (s ^ flag[0])] = (
+            summed[0:height, count * s : count * (s + 1)]
+            * factors[1 + s]
+            * lax.rsqrt(norm / total + epsilon)
         )
 
 
@@ -267,6 +294,9 @@
 
     def self_call(*refs):
         self_kernel(total, *refs)
+
+    def left_call(*refs):
+        left_kernel(total, *refs)
 
     def last_call(*refs):
         last_kernel(total, *refs)
@@ -294,7 +324,10 @@
     scratch = [pltpu.VMEM((count, 2 * class_count), f32)]
 
     def fetch(bits):
-        pairs = [one_way(blocks, voxes, bit) for bit in bits]
+        pairs = [
+            (both_cores if whole else one_way)(blocks, voxes, bit)
+            for bit, whole in zip(bits, sent_whole(bits))
+        ]
 
         def run(left, rows, labels, place):
             blocks_in = [lax.ppermute(left, axes, pair) for pair in pairs]
@@ -324,10 +357,26 @@
         return run
 
     def give_back(bits):
-        return lambda *sent: tuple(
-            lax.ppermute(part, axes, back(one_way(blocks, voxes, bit)))
-            for part, bit in zip(sent, bits)
-        )
+        whole = sent_whole(bits)
+
+        def merge_call(*refs):
+            merge_kernel(whole, *refs)
+
+        def run(own, first_partial, second_partial, *sent):
+            received = [
+                lax.ppermute(part, axes, back(one_way(blocks, voxes, bit)))
+                for part, bit, all_sent in zip(sent, bits, whole)
+                if not all_sent
+            ]
+            return local_call(
+                merge_call,
+                shape((voxes, height + class_count, 2 * count), f32),
+                [in_vmem] * (3 + len(received)),
+                in_vmem,
+                (own, first_partial, second_partial, *received),
+            )
+
+        return run
 
     first, second, first_partial, second_partial, sums, self_out = lax.switch(
         index, [fetch(bits) for bits in bit_pairs], left, rows, labels, place
@@ -340,23 +389,30 @@
         (first, second, rows, left),
         [pltpu.VMEM((2, 2 * count, width), bf16), pltpu.SemaphoreType.DMA((4,))],
     )
-    first_back, second_back = lax.switch(
-        index, [give_back(bits) for bits in bit_pairs], first_sent, second_sent
-    )
-    merged = local_call(
-        merge_kernel,
-        shape((voxes, height + class_count, 2 * count), f32),
-        [in_vmem] * 5,
+    merged = lax.switch(
+        index,
+        [give_back(bits) for bits in bit_pairs],
+        own,
+        first_partial,
+        second_partial,
+        first_sent,
+        second_sent,
+    )
+    pieces = lax.all_to_all(merged, "vox", 0, 0, tiled=True)
+    factors = local_call(
+        left_call,
+        shape((3, height, count), f32),
+        [in_smem] + [in_vmem] * 5,
         in_vmem,
-        (own, first_back, second_back, first_partial, second_partial),
-    )
-    pieces = lax.all_to_all(merged, "vox", 0, 0, tiled=True)
+        (place, sums, labels, first_partial, second_partial, self_out),
+        [pltpu.VMEM((count, class_count), f32)],
+    )
     out = local_call(
         last_call,
         shape((3, height, count), f32),
-        [in_smem, in_smem] + [in_vmem] * 6,
+        [in_smem, in_smem] + [in_vmem] * 3,
         in_vmem,
-        (flag, place, pieces, sums, labels, first_partial, second_partial, self_out),
+        (flag, place, pieces, factors, labels),
         scratch,
     )
     return out.transpose(0, 2, 1)

time: 110 us -> 107 us (0.973)
  the two profiles are of different devices: /device:TPU:24 before, /device:TPU:1 now
where the time goes in v3:
time: 107 us; the launch traced here: 106 us
  starting transfers between devices  49.9 us (47%)
  waiting for transfers between devices  41.3 us (39%)
  Pallas kernels  12.7 us (12%)
    ppermute x2, waiting for transfers between devices, run(): lax.ppermute(partial, 'blk', both_ways(blocks, bit))  30.4 us
    all_to_all x1, starting transfers between devices, run(): message = lax.all_to_all(message, 'vox', 0, 0, tiled=True)  20.6 us
    all_to_all x1, starting transfers between devices, body(): pieces = lax.all_to_all(merged, 'vox', 0, 0, tiled=True)  13.5 us
    pallas_call x7, Pallas kernels, local_call(): pl.pallas_call(kernel, out_shape=out_shape, in_specs=in_specs, out_specs=...  12.7 us
    ppermute x2, starting transfers between devices, run(): blocks_in = [lax.ppermute(left, axes, pair) for pair in pairs]  6.95 us
    all_to_all x1, waiting for transfers between devices, body(): pieces = lax.all_to_all(merged, 'vox', 0, 0, tiled=True)  6.45 us
    ppermute x1, starting transfers between devices, run(): lax.ppermute(part, axes, back(one_way(blocks, voxes, bit)))  4.99 us
    ppermute x2, starting transfers between devices, run(): lax.ppermute(partial, 'blk', both_ways(blocks, bit))  3.87 us
  transfers between devices with their start and end apart: 7, of which 4 were waited for; matrix products, arithmetic and copies ran while one was open for 0% of the time, Pallas kernels for 3%

profile of v3, /device:TPU:1, one launch (start us, length us, event | category | flops | bytes accessed | tf_op | source)
XLA Modules:
  0.0 105.9 jit_solution(8243696842249690092)
XLA Ops:
  0.0 0.0 copy-start
  0.0 0.7 copy-done
  0.7 2.8 %shard_map.64 = (s32[1]{0:T(128)}, s32[1]{0:T(128)}, bf16[2,192,1280]{2,1,0:T(8,128)(2,1)S(1)}, f32[8,1280]{1,0:T(8,128)S(1)}) custom-call(bf16[192,2,1280]{2,1,0:T(2,128)(2,1)} %refs_0_.1, s32[192]{0:T(256)S(1)} %copy-done, s32[2,128]{1,0:T(2,128)} %refs_2_.1, s32[1280]{0:T(1024)} %refs_3_.1, s32[1280]{0:T(1024)} %refs_4_.1, f32[13]{0:T(128)} %refs_5_.1), custom_call_target="tpu_custom_call" | custom-call | tf_op jit(solution)/shard_map/pallas_call | solution.py:29
  4.1 67.2 %conditional.2 = (bf16[2,192,1280]{2,1,0:T(8,128)(2,1)}, bf16[2,192,1280]{2,1,0:T(8,128)(2,1)}, f32[16,192]{1,0:T(8,128)}, f32[16,192]{1,0:T(8,128)}, f32[8,192]{1,0:T(8,128)S(1)}, /*index=5*/f32[48,192]{1,0:T(8,128)S(1)}) conditional(s32[]{:T(128)} %bitcast.1, (bf16[2,192,1280]{2,1,0:T(8,128)(2,1)S(1)}, ...), branch_computations={%region_0.0_spmd, %region_1.0_spmd, %region_2.0_spmd, %region_3.0_... | conditional | bytes 8593648 | solution.py:381
  4.4 1.3 %collective-permute-start.69 = (bf16[2,192,1280]{2,1,0:T(8,128)(2,1)S(1)}, bf16[2,192,1280]{2,1,0:T(8,128)(2,1)}, u32[]{:S(2)}, u32[]{:S(2)}) collective-permute-start(bf16[2,192,1280]{2,1,0:T(8,128)(2,1)S(1)} %get-tuple-element.509.left), channel_id=1, source_target_pairs={{0,256},{2,258},{4,260},{6,262},{8,264},{10,266},{12,268},{14,270}... | collective-permute-start | bytes 2949128 | tf_op jit(solution)/shard_map/cond/branch_17_fun/ppermute | solution.py:333
  5.7 5.7 %collective-permute-start.68 = (bf16[2,192,1280]{2,1,0:T(8,128)(2,1)S(1)}, bf16[2,192,1280]{2,1,0:T(8,128)(2,1)}, u32[]{:S(2)}, u32[]{:S(2)}) collective-permute-start(bf16[2,192,1280]{2,1,0:T(8,128)(2,1)S(1)} %get-tuple-element.509.left), channel_id=1, source_target_pairs={{0,16},{1,17},{2,18},{3,19},{4,20},{5,21},{6,22},{7,23},{8,24},{9,... | collective-permute-start | bytes 2949128 | tf_op jit(solution)/shard_map/cond/branch_17_fun/ppermute | solution.py:333
  11.3 2.0 %branch_17_fun.3 = (f32[4,56,192]{2,1,0:T(8,128)}, f32[16,192]{1,0:T(8,128)S(1)}) custom-call(bf16[2,192,1280]{2,1,0:T(8,128)(2,1)S(1)} %get-tuple-element.509.left, f32[8,1280]{1,0:T(8,128)S(1)} %get-tuple-element.510.rows, s32[1,192]{1,0:T(1,128)S(1)} %get-tuple-element.511.labels.refs_2_), custom_call_target="tpu_custom_call" | custom-call | tf_op jit(solution)/shard_map/cond/branch_17_fun/pallas_call | solution.py:29
  13.3 20.6 %all-to-all-start.17 = ((f32[4,56,192]{2,1,0:T(8,128)}), f32[4,56,192]{2,1,0:T(8,128)S(1)}, u32[]{:S(2)}, u32[]{:S(2)}) async-start(f32[4,56,192]{2,1,0:T(8,128)} %get-tuple-element.514), calls=%async_computation.17 | async-start | bytes 458752 | tf_op jit(solution)/shard_map/cond/branch_17_fun/all_to_all | solution.py:346
  34.0 1.9 %collective-permute-start.71 = (f32[16,192]{1,0:T(8,128)S(1)}, f32[16,192]{1,0:T(8,128)}, u32[]{:S(2)}, u32[]{:S(2)}) collective-permute-start(f32[16,192]{1,0:T(8,128)S(1)} %get-tuple-element.512), channel_id=1, source_target_pairs={{0,256},{4,260},{8,264},{12,268},{16,272},{20,276},{24,280},{28,28... | collective-permute-start | bytes 36872 | tf_op jit(solution)/shard_map/cond/branch_17_fun/ppermute | solution.py:345
  35.9 2.0 %collective-permute-start.70 = (f32[16,192]{1,0:T(8,128)S(1)}, f32[16,192]{1,0:T(8,128)}, u32[]{:S(2)}, u32[]{:S(2)}) collective-permute-start(f32[16,192]{1,0:T(8,128)S(1)} %get-tuple-element.512), channel_id=1, source_target_pairs={{0,16},{4,20},{8,24},{12,28},{16,0},{20,4},{24,8},{28,12},{32,48},... | collective-permute-start | bytes 36872 | tf_op jit(solution)/shard_map/cond/branch_17_fun/ppermute | solution.py:345
  37.9 2.4 %all-to-all-done.17.refs_1_ = f32[4,56,192]{2,1,0:T(8,128)S(1)} async-done(((f32[4,56,192]{2,1,0:T(8,128)}), f32[4,56,192]{2,1,0:T(8,128)S(1)}, u32[]{:S(2)}, u32[]{:S(2)}) %all-to-all-start.17) | async-done | bytes 172064 | tf_op jit(solution)/shard_map/cond/branch_17_fun/all_to_all | solution.py:346
  40.3 0.4 branch_17_fun.4
  40.7 30.4 %collective-permute-done.71 = f32[16,192]{1,0:T(8,128)} collective-permute-done((f32[16,192]{1,0:T(8,128)S(1)}, f32[16,192]{1,0:T(8,128)}, u32[]{:S(2)}, u32[]{:S(2)}) %collective-permute-start.71) | collective-permute-done | bytes 12320 | tf_op jit(solution)/shard_map/cond/branch_17_fun/ppermute | solution.py:345
  71.1 0.0 collective-permute-done.70
  71.1 0.0 collective-permute-done.69
  71.1 0.0 collective-permute-done.68
  71.3 2.9 %shard_map.65 = (f32[2,192,192]{2,1,0:T(8,128)S(1)}, f32[96,384]{1,0:T(8,128)S(1)}, f32[96,384]{1,0:T(8,128)S(1)}) custom-call(bf16[2,192,1280]{2,1,0:T(8,128)(2,1)} %get-tuple-element.647.first, bf16[2,192,1280]{2,1,0:T(8,128)(2,1)} %get-tuple-element.648.second, f32[8,1280]{1,0:T(8,128)S(1)} %get-tuple-element.646.rows, ...), custom_call_target="tpu_custom_call" | custom-call | tf_op jit(solution)/shard_map/pallas_call | solution.py:29
  74.3 8.8 %conditional.3 = (f32[4,56,384]{2,1,0:T(8,128)}) conditional(s32[]{:T(128)} %bitcast.1, (f32[2,192,192]{2,1,0:T(8,128)S(1)}, f32[16,192]{1,0:T(8,128)}, f32[16,192]{1,0:T(8,128)}) %tuple.153, (f32[2,192,192]{2,1,0:T(8,128)S(1)}, f32[16,192]{1,0:T(8,128)}, f32[16,192]{1,0:T(8,128)}) %tuple.153, ...), branch_computations={%region_21.0_spmd, %region_22.0_spmd, %region_23.0_spmd, %region_2... | conditional | bytes 1179736 | solution.py:392
  74.3 5.0 %collective-permute-start.103 = (f32[96,384]{1,0:T(8,128)S(1)}, f32[96,384]{1,0:T(8,128)S(1)}, u32[]{:S(2)}, u32[]{:S(2)}) collective-permute-start(f32[96,384]{1,0:T(8,128)S(1)} %get-tuple-element.614), channel_id=1, source_target_pairs={{256,0},{258,2},{260,4},{262,6},{264,8},{266,10},{268,12},{270,14}... | collective-permute-start | bytes 442376 | tf_op jit(solution)/shard_map/cond/branch_17_fun/ppermute | solution.py:367
  79.3 2.1 %collective-permute-done.103.refs_3_ = f32[96,384]{1,0:T(8,128)S(1)} collective-permute-done((f32[96,384]{1,0:T(8,128)S(1)}, f32[96,384]{1,0:T(8,128)S(1)}, u32[]{:S(2)}, u32[]{:S(2)}) %collective-permute-start.103) | collective-permute-done | bytes 147488 | tf_op jit(solution)/shard_map/cond/branch_17_fun/ppermute | solution.py:367
  81.4 1.6 %branch_17_fun.5 = f32[4,56,384]{2,1,0:T(8,128)} custom-call(f32[2,192,192]{2,1,0:T(8,128)S(1)} %get-tuple-element.611.refs_0_, f32[16,192]{1,0:T(8,128)} %get-tuple-element.612.refs_1_, f32[16,192]{1,0:T(8,128)} %get-tuple-element.613.refs_2_, f32[96,384]{1,0:T(8,128)S(1)} %collective-permute-done.103.refs_3_), custom_call_target="tpu_custom_call" | custom-call | tf_op jit(solution)/shard_map/cond/branch_17_fun/pallas_call | solution.py:29
  83.0 13.5 %all-to-all-start.21 = ((f32[4,56,384]{2,1,0:T(8,128)}), f32[4,56,384]{2,1,0:T(8,128)S(1)}, u32[]{:S(2)}, u32[]{:S(2)}) async-start(f32[4,56,384]{2,1,0:T(8,128)} %get-tuple-element.782), calls=%async_computation.21 | async-start | bytes 688128 | tf_op jit(solution)/shard_map/all_to_all | solution.py:401
  96.5 1.1 %shard_map.66.refs_3_ = f32[3,48,192]{2,1,0:T(8,128)S(1)} custom-call(s32[1]{0:T(128)} %bitcast.refs_0_.refs_1_, f32[8,192]{1,0:T(8,128)S(1)} %get-tuple-element.654.refs_1_, s32[1,192]{1,0:T(1,128)S(1)} %bitcast.25, f32[16,192]{1,0:T(8,128)} %get-tuple-element.650.refs_3_, f32[16,192]{1,0:T(8,128)} %get-tuple-element.651.refs_4_, ...), custom_call_target="tpu_custom_call" | custom-call | tf_op jit(solution)/shard_map/pallas_call | solution.py:29
  97.6 6.5 %all-to-all-done.21.refs_2_ = f32[4,56,384]{2,1,0:T(8,128)S(1)} async-done(((f32[4,56,384]{2,1,0:T(8,128)}), f32[4,56,384]{2,1,0:T(8,128)S(1)}, u32[]{:S(2)}, u32[]{:S(2)}) %all-to-all-start.21) | async-done | bytes 344096 | tf_op jit(solution)/shard_map/all_to_all | solution.py:401
  104.1 1.9 %shard_map.67 = f32[3,48,192]{2,1,0:T(8,128)} custom-call(s32[1]{0:T(128)} %get-tuple-element.643.refs_0_, s32[1]{0:T(128)} %bitcast.refs_0_.refs_1_, f32[4,56,384]{2,1,0:T(8,128)S(1)} %all-to-all-done.21.refs_2_, f32[3,48,192]{2,1,0:T(8,128)S(1)} %shard_map.66.refs_3_, s32[1,192]{1,0:T(1,128)S(1)} %bitcast.26), custom_call_target="tpu_custom_call" | custom-call | tf_op jit(solution)/shard_map/pallas_call | solution.py:29
Async XLA Ops:
  0.0 0.7 copy-start
  4.4 66.7 %collective-permute-start.69 = (bf16[2,192,1280]{2,1,0:T(8,128)(2,1)S(1)}, bf16[2,192,1280]{2,1,0:T(8,128)(2,1)}, u32[]{:S(2)}, u32[]{:S(2)}) collective-permute-start(bf16[2,192,1280]{2,1,0:T(8,128)(2,1)S(1)} %get-tuple-element.509.left), channel_id=1, source_target_pairs={{0,256},{2,258},{4,260},{6,262},{8,264},{10,266},{12,268},{14,270}... | collective-permute-start | bytes 2949128 | tf_op jit(solution)/shard_map/cond/branch_17_fun/ppermute | solution.py:333
  5.7 65.4 %collective-permute-start.68 = (bf16[2,192,1280]{2,1,0:T(8,128)(2,1)S(1)}, bf16[2,192,1280]{2,1,0:T(8,128)(2,1)}, u32[]{:S(2)}, u32[]{:S(2)}) collective-permute-start(bf16[2,192,1280]{2,1,0:T(8,128)(2,1)S(1)} %get-tuple-element.509.left), channel_id=1, source_target_pairs={{0,16},{1,17},{2,18},{3,19},{4,20},{5,21},{6,22},{7,23},{8,24},{9,... | collective-permute-start | bytes 2949128 | tf_op jit(solution)/shard_map/cond/branch_17_fun/ppermute | solution.py:333
  13.3 27.0 %all-to-all-start.17 = ((f32[4,56,192]{2,1,0:T(8,128)}), f32[4,56,192]{2,1,0:T(8,128)S(1)}, u32[]{:S(2)}, u32[]{:S(2)}) async-start(f32[4,56,192]{2,1,0:T(8,128)} %get-tuple-element.514), calls=%async_computation.17 | async-start | bytes 458752 | tf_op jit(solution)/shard_map/cond/branch_17_fun/all_to_all | solution.py:346
  34.0 37.1 %collective-permute-start.71 = (f32[16,192]{1,0:T(8,128)S(1)}, f32[16,192]{1,0:T(8,128)}, u32[]{:S(2)}, u32[]{:S(2)}) collective-permute-start(f32[16,192]{1,0:T(8,128)S(1)} %get-tuple-element.512), channel_id=1, source_target_pairs={{0,256},{4,260},{8,264},{12,268},{16,272},{20,276},{24,280},{28,28... | collective-permute-start | bytes 36872 | tf_op jit(solution)/shard_map/cond/branch_17_fun/ppermute | solution.py:345
  35.9 35.2 %collective-permute-start.70 = (f32[16,192]{1,0:T(8,128)S(1)}, f32[16,192]{1,0:T(8,128)}, u32[]{:S(2)}, u32[]{:S(2)}) collective-permute-start(f32[16,192]{1,0:T(8,128)S(1)} %get-tuple-element.512), channel_id=1, source_target_pairs={{0,16},{4,20},{8,24},{12,28},{16,0},{20,4},{24,8},{28,12},{32,48},... | collective-permute-start | bytes 36872 | tf_op jit(solution)/shard_map/cond/branch_17_fun/ppermute | solution.py:345
  74.3 7.1 %collective-permute-start.103 = (f32[96,384]{1,0:T(8,128)S(1)}, f32[96,384]{1,0:T(8,128)S(1)}, u32[]{:S(2)}, u32[]{:S(2)}) collective-permute-start(f32[96,384]{1,0:T(8,128)S(1)} %get-tuple-element.614), channel_id=1, source_target_pairs={{256,0},{258,2},{260,4},{262,6},{264,8},{266,10},{268,12},{270,14}... | collective-permute-start | bytes 442376 | tf_op jit(solution)/shard_map/cond/branch_17_fun/ppermute | solution.py:367
  83.0 21.0 %all-to-all-start.21 = ((f32[4,56,384]{2,1,0:T(8,128)}), f32[4,56,384]{2,1,0:T(8,128)S(1)}, u32[]{:S(2)}, u32[]{:S(2)}) async-start(f32[4,56,384]{2,1,0:T(8,128)} %get-tuple-element.782), calls=%async_computation.21 | async-start | bytes 688128 | tf_op jit(solution)/shard_map/all_to_all | solution.py:401

commit v4 on v3

--- a/solution.py
+++ b/solution.py
@@ -81,9 +81,9 @@
 
 
 def mask_kernel(
-    bit_count, x, labels, plan, shells, angles, gain, index_out, flag_out, left_out, *scratch
+    bit_count, x, labels, plan, shells, angles, gain, index_out, flag_out, left_out, rows, labels_out, *scratch
 ):
-    rows, buffers, sems = scratch[0], scratch[1:-1], scratch[-1]
+    buffers, sems = scratch[:-1], scratch[-1]
     half = left_out.shape[1] // 2
     block, labels_in, plan_in, shells_in, angles_in, gain_in = buffers
     halves = [
@@ -118,22 +118,16 @@
         weights = jnp.where(shell_row == s + first_shell, gain_in[s], weights)
     rows[0:1, :] = weights.astype(bf16).astype(f32)
     rows[1:2, :] = angle_row
-    limits = limits_of(labels_in[...].reshape(1, -1)).astype(bf16)
-    chunk = chunk_of(x.shape[2])
+    labels_out[...] = labels_in[...].reshape(1, -1)
+    limits = limits_of(labels_out[...]).astype(bf16)
+    angle_row = angle_row.astype(bf16)
     for h in range(2):
         halves[h].wait()
-
-        def step(i, carry):
-            at = pl.ds(pl.multiple_of(i * chunk, chunk), chunk)
-            keep = jnp.clip(
-                limits[half * h : half * (h + 1)] - rows[1:2, at].astype(bf16), 0, 1
-            )
-            parts = jnp.swapaxes(block[half * h : half * (h + 1), :, at], 0, 1)
-            for t in range(2):
-                left_out[t, half * h : half * (h + 1), at] = parts[t] * keep
-            return carry
-
-        lax.fori_loop(0, x.shape[2] // chunk, step, 0)
+        down = slice(half * h, half * (h + 1))
+        keep = jnp.clip(limits[down] - angle_row, 0, 1)
+        parts = jnp.swapaxes(block[down], 0, 1)
+        for t in range(2):
+            left_out[t, down, :] = parts[t] * keep
 
 
 def own_kernel(left, rows, labels, message, partial, acc, sums):
@@ -302,19 +296,19 @@
         last_kernel(total, *refs)
 
     place = lax.axis_index("vox").reshape(1)
-    labels = classes.reshape(1, -1)
     arrays = (particles, classes, plan, voxel_shell, voxel_angle, shell_gain)
     spaces = (pltpu.VMEM, pltpu.VMEM, pltpu.SMEM, pltpu.VMEM, pltpu.VMEM, pltpu.SMEM)
-    index, flag, left, rows = local_call(
+    index, flag, left, rows, labels = local_call(
         mask_call,
         (
             shape((1,), jnp.int32),
             shape((1,), jnp.int32),
             shape((2, count, width), bf16),
             shape((8, width), f32),
+            shape((1, count), jnp.int32),
         ),
         [in_hbm] * len(arrays),
-        (in_smem, in_smem, in_vmem, in_vmem),
+        (in_smem, in_smem) + (in_vmem,) * 3,
         arrays,
         [space(array.shape, array.dtype) for space, array in zip(spaces, arrays)]
         + [pltpu.SemaphoreType.DMA((1 + len(arrays),))],

time: 107 us -> 56.5 us (0.53)
  waiting for transfers between devices: 41.3 us -> 16.7 us
  starting transfers between devices: 49.9 us -> 26.1 us
    ppermute x2, waiting for transfers between devices: 30.4 us -> 0.01 us  [run(): lax.ppermute(partial, 'blk', both_ways(blocks, bit))]
    all_to_all x1, starting transfers between devices: 20.6 us -> 6.92 us  [run(): message = lax.all_to_all(message, 'vox', 0, 0, tiled=True)]
    all_to_all x1, starting transfers between devices: 13.5 us -> 4.73 us  [body(): pieces = lax.all_to_all(merged, 'vox', 0, 0, tiled=True)]
    all_to_all x1, waiting for transfers between devices: 2.43 us -> 10.3 us  [run(): message = lax.all_to_all(message, 'vox', 0, 0, tiled=True)]
    ppermute x1 -> x0, starting transfers between devices: 4.99 us -> none  [run(): lax.ppermute(part, axes, back(one_way(blocks, voxes, bit)))]
    ppermute x2, starting transfers between devices: 3.87 us -> 7.27 us  [run(): lax.ppermute(partial, 'blk', both_ways(blocks, bit))]
    ppermute x1 -> x0, waiting for transfers between devices: 2.08 us -> none  [run(): lax.ppermute(part, axes, back(one_way(blocks, voxes, bit)))]
  transfers between devices with their start and end apart: 7 -> 6, of which waited for: 4 -> 2; matrix products, arithmetic and copies ran while one was open for 0% -> 0% of each run, Pallas kernels for 3% -> 6%
where the time goes in v4:
time: 56.5 us; the launch traced here: 55.8 us
  starting transfers between devices  26.1 us (46%)
  waiting for transfers between devices  16.7 us (30%)
  Pallas kernels  11.9 us (21%)
  between operations  0.68 us (1%)
    pallas_call x7, Pallas kernels, local_call(): pl.pallas_call(kernel, out_shape=out_shape, in_specs=in_specs, out_specs=...  11.9 us
    all_to_all x1, waiting for transfers between devices, run(): message = lax.all_to_all(message, 'vox', 0, 0, tiled=True)  10.3 us
    ppermute x2, starting transfers between devices, run(): lax.ppermute(partial, 'blk', both_ways(blocks, bit))  7.27 us
    ppermute x2, starting transfers between devices, run(): blocks_in = [lax.ppermute(left, axes, pair) for pair in pairs]  7.16 us
    all_to_all x1, starting transfers between devices, run(): message = lax.all_to_all(message, 'vox', 0, 0, tiled=True)  6.92 us
    all_to_all x1, waiting for transfers between devices, body(): pieces = lax.all_to_all(merged, 'vox', 0, 0, tiled=True)  6.46 us
    all_to_all x1, starting transfers between devices, body(): pieces = lax.all_to_all(merged, 'vox', 0, 0, tiled=True)  4.73 us
  transfers between devices with their start and end apart: 6, of which 2 were waited for; matrix products, arithmetic and copies ran while one was open for 0% of the time, Pallas kernels for 6%

profile of v4, /device:TPU:1, one launch (start us, length us, event | category | flops | bytes accessed | tf_op | source)
XLA Modules:
  0.0 55.8 jit_solution(16929731629598098477)
XLA Ops:
  0.0 2.0 %shard_map.64 = (s32[1]{0:T(128)}, s32[1]{0:T(128)}, bf16[2,192,1280]{2,1,0:T(8,128)(2,1)S(1)}, f32[8,1280]{1,0:T(8,128)S(1)}, s32[1,192]{1,0:T(1,128)S(1)}) custom-call(bf16[192,2,1280]{2,1,0:T(2,128)(2,1)} %refs_0_.1, s32[192]{0:T(256)} %refs_1_.1, s32[2,128]{1,0:T(2,128)} %refs_2_.1, s32[1280]{0:T(1024)} %refs_3_.1, s32[1280]{0:T(1024)} %refs_4_.1, f32[13]{0:T(128)} %refs_5_.1), custom_call_target="tpu_custom_call" | custom-call | tf_op jit(solution)/shard_map/pallas_call | solution.py:29
  2.6 34.3 %conditional.2 = (bf16[2,192,1280]{2,1,0:T(8,128)(2,1)}, bf16[2,192,1280]{2,1,0:T(8,128)(2,1)}, f32[16,192]{1,0:T(8,128)}, f32[16,192]{1,0:T(8,128)}, f32[8,192]{1,0:T(8,128)S(1)}, /*index=5*/f32[48,192]{1,0:T(8,128)S(1)}) conditional(s32[]{:T(128)} %bitcast.1, (bf16[2,192,1280]{2,1,0:T(8,128)(2,1)S(1)}, ...), branch_computations={%region_0.0_spmd, %region_1.0_spmd, %region_2.0_spmd, %region_3.0_... | conditional | bytes 8593648 | solution.py:375
  2.6 4.0 %collective-permute-start.1 = (bf16[2,192,1280]{2,1,0:T(8,128)(2,1)S(1)}, bf16[2,192,1280]{2,1,0:T(8,128)(2,1)}, u32[]{:S(2)}, u32[]{:S(2)}) collective-permute-start(bf16[2,192,1280]{2,1,0:T(8,128)(2,1)S(1)} %get-tuple-element.353.left), channel_id=1, source_target_pairs={{0,8},{1,9},{2,10},{3,11},{4,12},{5,13},{6,14},{7,15},{8,0},{9,1},... | collective-permute-start | bytes 2949128 | tf_op jit(solution)/shard_map/cond/branch_0_fun/ppermute | solution.py:327
  6.7 3.1 %collective-permute-start = (bf16[2,192,1280]{2,1,0:T(8,128)(2,1)S(1)}, bf16[2,192,1280]{2,1,0:T(8,128)(2,1)}, u32[]{:S(2)}, u32[]{:S(2)}) collective-permute-start(bf16[2,192,1280]{2,1,0:T(8,128)(2,1)S(1)} %get-tuple-element.353.left), channel_id=1, source_target_pairs={{0,4},{1,5},{2,6},{3,7},{4,0},{5,1},{6,2},{7,3},{8,12},{9,13},{10,... | collective-permute-start | bytes 2949128 | tf_op jit(solution)/shard_map/cond/branch_0_fun/ppermute | solution.py:327
  9.8 2.0 %branch_0_fun.3 = (f32[4,56,192]{2,1,0:T(8,128)}, f32[16,192]{1,0:T(8,128)S(1)}) custom-call(bf16[2,192,1280]{2,1,0:T(8,128)(2,1)S(1)} %get-tuple-element.353.left, f32[8,1280]{1,0:T(8,128)S(1)} %get-tuple-element.354.rows, s32[1,192]{1,0:T(1,128)S(1)} %get-tuple-element.355.labels.refs_2_), custom_call_target="tpu_custom_call" | custom-call | tf_op jit(solution)/shard_map/cond/branch_0_fun/pallas_call | solution.py:29
  11.8 6.9 %all-to-all-start = ((f32[4,56,192]{2,1,0:T(8,128)}), f32[4,56,192]{2,1,0:T(8,128)S(1)}, u32[]{:S(2)}, u32[]{:S(2)}) async-start(f32[4,56,192]{2,1,0:T(8,128)} %get-tuple-element.364), calls=%async_computation | async-start | bytes 458752 | tf_op jit(solution)/shard_map/cond/branch_0_fun/all_to_all | solution.py:340
  18.7 3.6 %collective-permute-start.3 = (f32[16,192]{1,0:T(8,128)S(1)}, f32[16,192]{1,0:T(8,128)}, u32[]{:S(2)}, u32[]{:S(2)}) collective-permute-start(f32[16,192]{1,0:T(8,128)S(1)} %get-tuple-element.356), channel_id=1, source_target_pairs={{0,8},{4,12},{8,0},{12,4},{16,24},{20,28},{24,16},{28,20},{32,40},... | collective-permute-start | bytes 36872 | tf_op jit(solution)/shard_map/cond/branch_0_fun/ppermute | solution.py:339
  22.4 3.6 %collective-permute-start.2 = (f32[16,192]{1,0:T(8,128)S(1)}, f32[16,192]{1,0:T(8,128)}, u32[]{:S(2)}, u32[]{:S(2)}) collective-permute-start(f32[16,192]{1,0:T(8,128)S(1)} %get-tuple-element.356), channel_id=1, source_target_pairs={{0,4},{4,0},{8,12},{12,8},{16,20},{20,16},{24,28},{28,24},{32,36},... | collective-permute-start | bytes 36872 | tf_op jit(solution)/shard_map/cond/branch_0_fun/ppermute | solution.py:339
  26.0 10.3 %all-to-all-done.refs_1_ = f32[4,56,192]{2,1,0:T(8,128)S(1)} async-done(((f32[4,56,192]{2,1,0:T(8,128)}), f32[4,56,192]{2,1,0:T(8,128)S(1)}, u32[]{:S(2)}, u32[]{:S(2)}) %all-to-all-start) | async-done | bytes 172064 | tf_op jit(solution)/shard_map/cond/branch_0_fun/all_to_all | solution.py:340
  36.3 0.4 branch_0_fun.4
  36.7 0.0 collective-permute-done.3
  36.7 0.0 collective-permute-done.2
  36.7 0.0 collective-permute-done.1
  36.7 0.0 collective-permute-done
  37.0 2.9 %shard_map.65 = (f32[2,192,192]{2,1,0:T(8,128)S(1)}, f32[96,384]{1,0:T(8,128)S(1)}, f32[96,384]{1,0:T(8,128)S(1)}) custom-call(bf16[2,192,1280]{2,1,0:T(8,128)(2,1)} %get-tuple-element.649.first, bf16[2,192,1280]{2,1,0:T(8,128)(2,1)} %get-tuple-element.650.second, f32[8,1280]{1,0:T(8,128)S(1)} %get-tuple-element.647.rows, ...), custom_call_target="tpu_custom_call" | custom-call | tf_op jit(solution)/shard_map/pallas_call | solution.py:29
  39.9 1.6 %conditional.3 = (f32[4,56,384]{2,1,0:T(8,128)}) conditional(s32[]{:T(128)} %bitcast.1, (f32[2,192,192]{2,1,0:T(8,128)S(1)}, f32[16,192]{1,0:T(8,128)}, f32[16,192]{1,0:T(8,128)}) %tuple.153, (f32[2,192,192]{2,1,0:T(8,128)S(1)}, f32[16,192]{1,0:T(8,128)}, f32[16,192]{1,0:T(8,128)}) %tuple.153, ...), branch_computations={%region_21.0_spmd, %region_22.0_spmd, %region_23.0_spmd, %region_2... | conditional | bytes 1179736 | solution.py:386
  39.9 1.6 %branch_0_fun.5 = f32[4,56,384]{2,1,0:T(8,128)} custom-call(f32[2,192,192]{2,1,0:T(8,128)S(1)} %get-tuple-element.541.refs_0_, f32[16,192]{1,0:T(8,128)} %get-tuple-element.542.refs_1_, f32[16,192]{1,0:T(8,128)} %get-tuple-element.543.refs_2_), custom_call_target="tpu_custom_call" | custom-call | tf_op jit(solution)/shard_map/cond/branch_0_fun/pallas_call | solution.py:29
  41.5 4.7 %all-to-all-start.21 = ((f32[4,56,384]{2,1,0:T(8,128)}), f32[4,56,384]{2,1,0:T(8,128)S(1)}, u32[]{:S(2)}, u32[]{:S(2)}) async-start(f32[4,56,384]{2,1,0:T(8,128)} %get-tuple-element.784), calls=%async_computation.21 | async-start | bytes 688128 | tf_op jit(solution)/shard_map/all_to_all | solution.py:395
  46.3 1.1 %shard_map.66.refs_3_ = f32[3,48,192]{2,1,0:T(8,128)S(1)} custom-call(s32[1]{0:T(128)} %bitcast.refs_0_.refs_1_, f32[8,192]{1,0:T(8,128)S(1)} %get-tuple-element.656.refs_1_, s32[1,192]{1,0:T(1,128)S(1)} %get-tuple-element.648.refs_2_.refs_4_, f32[16,192]{1,0:T(8,128)} %get-tuple-element.652.refs_3_, f32[16,192]{1,0:T(8,128)} %get-tuple-element.653.refs_4_, ...), custom_call_target="tpu_custom_call" | custom-call | tf_op jit(solution)/shard_map/pallas_call | solution.py:29
  47.4 6.5 %all-to-all-done.21.refs_2_ = f32[4,56,384]{2,1,0:T(8,128)S(1)} async-done(((f32[4,56,384]{2,1,0:T(8,128)}), f32[4,56,384]{2,1,0:T(8,128)S(1)}, u32[]{:S(2)}, u32[]{:S(2)}) %all-to-all-start.21) | async-done | bytes 344096 | tf_op jit(solution)/shard_map/all_to_all | solution.py:395
  53.8 2.0 %shard_map.67 = f32[3,48,192]{2,1,0:T(8,128)} custom-call(s32[1]{0:T(128)} %get-tuple-element.644.refs_0_, s32[1]{0:T(128)} %bitcast.refs_0_.refs_1_, f32[4,56,384]{2,1,0:T(8,128)S(1)} %all-to-all-done.21.refs_2_, f32[3,48,192]{2,1,0:T(8,128)S(1)} %shard_map.66.refs_3_, s32[1,192]{1,0:T(1,128)S(1)} %get-tuple-element.648.refs_2_.refs_4_), custom_call_target="tpu_custom_call" | custom-call | tf_op jit(solution)/shard_map/pallas_call | solution.py:29
Async XLA Ops:
  2.6 34.1 %collective-permute-start.1 = (bf16[2,192,1280]{2,1,0:T(8,128)(2,1)S(1)}, bf16[2,192,1280]{2,1,0:T(8,128)(2,1)}, u32[]{:S(2)}, u32[]{:S(2)}) collective-permute-start(bf16[2,192,1280]{2,1,0:T(8,128)(2,1)S(1)} %get-tuple-element.353.left), channel_id=1, source_target_pairs={{0,8},{1,9},{2,10},{3,11},{4,12},{5,13},{6,14},{7,15},{8,0},{9,1},... | collective-permute-start | bytes 2949128 | tf_op jit(solution)/shard_map/cond/branch_0_fun/ppermute | solution.py:327
  6.7 30.0 %collective-permute-start = (bf16[2,192,1280]{2,1,0:T(8,128)(2,1)S(1)}, bf16[2,192,1280]{2,1,0:T(8,128)(2,1)}, u32[]{:S(2)}, u32[]{:S(2)}) collective-permute-start(bf16[2,192,1280]{2,1,0:T(8,128)(2,1)S(1)} %get-tuple-element.353.left), channel_id=1, source_target_pairs={{0,4},{1,5},{2,6},{3,7},{4,0},{5,1},{6,2},{7,3},{8,12},{9,13},{10,... | collective-permute-start | bytes 2949128 | tf_op jit(solution)/shard_map/cond/branch_0_fun/ppermute | solution.py:327
  11.8 24.5 %all-to-all-start = ((f32[4,56,192]{2,1,0:T(8,128)}), f32[4,56,192]{2,1,0:T(8,128)S(1)}, u32[]{:S(2)}, u32[]{:S(2)}) async-start(f32[4,56,192]{2,1,0:T(8,128)} %get-tuple-element.364), calls=%async_computation | async-start | bytes 458752 | tf_op jit(solution)/shard_map/cond/branch_0_fun/all_to_all | solution.py:340
  18.7 18.0 %collective-permute-start.3 = (f32[16,192]{1,0:T(8,128)S(1)}, f32[16,192]{1,0:T(8,128)}, u32[]{:S(2)}, u32[]{:S(2)}) collective-permute-start(f32[16,192]{1,0:T(8,128)S(1)} %get-tuple-element.356), channel_id=1, source_target_pairs={{0,8},{4,12},{8,0},{12,4},{16,24},{20,28},{24,16},{28,20},{32,40},... | collective-permute-start | bytes 36872 | tf_op jit(solution)/shard_map/cond/branch_0_fun/ppermute | solution.py:339
  22.4 14.3 %collective-permute-start.2 = (f32[16,192]{1,0:T(8,128)S(1)}, f32[16,192]{1,0:T(8,128)}, u32[]{:S(2)}, u32[]{:S(2)}) collective-permute-start(f32[16,192]{1,0:T(8,128)S(1)} %get-tuple-element.356), channel_id=1, source_target_pairs={{0,4},{4,0},{8,12},{12,8},{16,20},{20,16},{24,28},{28,24},{32,36},... | collective-permute-start | bytes 36872 | tf_op jit(solution)/shard_map/cond/branch_0_fun/ppermute | solution.py:339
  41.5 12.3 %all-to-all-start.21 = ((f32[4,56,384]{2,1,0:T(8,128)}), f32[4,56,384]{2,1,0:T(8,128)S(1)}, u32[]{:S(2)}, u32[]{:S(2)}) async-start(f32[4,56,384]{2,1,0:T(8,128)} %get-tuple-element.784), calls=%async_computation.21 | async-start | bytes 688128 | tf_op jit(solution)/shard_map/all_to_all | solution.py:395

commit v5 on v4

--- a/solution.py
+++ b/solution.py
@@ -57,7 +57,7 @@
 
 def sent_whole(bits):
     axis = [0 if bit == 0 else 1 if bit < 3 else 2 for bit in bits]
-    return tuple(axis[0] != axis[1] and bit < 4 and bits[1] != 4 for bit in bits)
+    return tuple(axis[0] != axis[1] and bit < 4 and bits != (0, 4) for bit in bits)
 
 
 def back(pairs):

time: 56.5 us -> 91 us (1.61)
  waiting for transfers between devices: 16.7 us -> 35.5 us
  starting transfers between devices: 26.1 us -> 41.5 us
    ppermute x2, waiting for transfers between devices: 0.01 us -> 24.5 us  [run(): lax.ppermute(partial, 'blk', both_ways(blocks, bit))]
    all_to_all x1, starting transfers between devices: 6.92 us -> 19.4 us  [run(): message = lax.all_to_all(message, 'vox', 0, 0, tiled=True)]
    ppermute x0 -> x2, starting transfers between devices: none -> 11.5 us  [run(): lax.ppermute(part, axes, back(one_way(blocks, voxes, bit)))]
    all_to_all x1, waiting for transfers between devices: 10.3 us -> 2.47 us  [run(): message = lax.all_to_all(message, 'vox', 0, 0, tiled=True)]
    ppermute x2, starting transfers between devices: 7.16 us -> 2.58 us  [run(): blocks_in = [lax.ppermute(left, axes, pair) for pair in pairs]]
    ppermute x2, starting transfers between devices: 7.27 us -> 3.83 us  [run(): lax.ppermute(partial, 'blk', both_ways(blocks, bit))]
    ppermute x0 -> x2, waiting for transfers between devices: none -> 2.07 us  [run(): lax.ppermute(part, axes, back(one_way(blocks, voxes, bit)))]
  transfers between devices with their start and end apart: 6 -> 8, of which waited for: 2 -> 4; matrix products, arithmetic and copies ran while one was open for 0% -> 0% of each run, Pallas kernels for 6% -> 4%
where the time goes in v5:
time: 91 us; the launch traced here: 90.2 us
  starting transfers between devices  41.5 us (46%)
  waiting for transfers between devices  35.5 us (39%)
  Pallas kernels  11.9 us (13%)
    ppermute x2, waiting for transfers between devices, run(): lax.ppermute(partial, 'blk', both_ways(blocks, bit))  24.5 us
    all_to_all x1, starting transfers between devices, run(): message = lax.all_to_all(message, 'vox', 0, 0, tiled=True)  19.4 us
    pallas_call x7, Pallas kernels, local_call(): pl.pallas_call(kernel, out_shape=out_shape, in_specs=in_specs, out_specs=...  11.9 us
    ppermute x2, starting transfers between devices, run(): lax.ppermute(part, axes, back(one_way(blocks, voxes, bit)))  11.5 us
    all_to_all x1, waiting for transfers between devices, body(): pieces = lax.all_to_all(merged, 'vox', 0, 0, tiled=True)  6.45 us
    all_to_all x1, starting transfers between devices, body(): pieces = lax.all_to_all(merged, 'vox', 0, 0, tiled=True)  4.24 us
    ppermute x2, starting transfers between devices, run(): lax.ppermute(partial, 'blk', both_ways(blocks, bit))  3.83 us
    ppermute x2, starting transfers between devices, run(): blocks_in = [lax.ppermute(left, axes, pair) for pair in pairs]  2.58 us
  transfers between devices with their start and end apart: 8, of which 4 were waited for; matrix products, arithmetic and copies ran while one was open for 0% of the time, Pallas kernels for 4%

profile of v5, /device:TPU:1, one launch (start us, length us, event | category | flops | bytes accessed | tf_op | source)
XLA Modules:
  0.0 90.2 jit_solution(11465389894024527319)
XLA Ops:
  0.0 2.0 %shard_map.64 = (s32[1]{0:T(128)}, s32[1]{0:T(128)}, bf16[2,192,1280]{2,1,0:T(8,128)(2,1)S(1)}, f32[8,1280]{1,0:T(8,128)S(1)}, s32[1,192]{1,0:T(1,128)S(1)}) custom-call(bf16[192,2,1280]{2,1,0:T(2,128)(2,1)} %refs_0_.1, s32[192]{0:T(256)} %refs_1_.1, s32[2,128]{1,0:T(2,128)} %refs_2_.1, s32[1280]{0:T(1024)} %refs_3_.1, s32[1280]{0:T(1024)} %refs_4_.1, f32[13]{0:T(128)} %refs_5_.1), custom_call_target="tpu_custom_call" | custom-call | tf_op jit(solution)/shard_map/pallas_call | solution.py:29
  2.6 55.7 %conditional.2 = (bf16[2,192,1280]{2,1,0:T(8,128)(2,1)}, bf16[2,192,1280]{2,1,0:T(8,128)(2,1)}, f32[16,192]{1,0:T(8,128)}, f32[16,192]{1,0:T(8,128)}, f32[8,192]{1,0:T(8,128)S(1)}, /*index=5*/f32[48,192]{1,0:T(8,128)S(1)}) conditional(s32[]{:T(128)} %bitcast.1, (bf16[2,192,1280]{2,1,0:T(8,128)(2,1)S(1)}, ...), branch_computations={%region_0.0_spmd, %region_1.0_spmd, %region_2.0_spmd, %region_3.0_... | conditional | bytes 8593648 | solution.py:375
  2.7 1.3 %collective-permute-start.57 = (bf16[2,192,1280]{2,1,0:T(8,128)(2,1)S(1)}, bf16[2,192,1280]{2,1,0:T(8,128)(2,1)}, u32[]{:S(2)}, u32[]{:S(2)}) collective-permute-start(bf16[2,192,1280]{2,1,0:T(8,128)(2,1)S(1)} %get-tuple-element.481.left), channel_id=1, source_target_pairs={{0,128},{2,130},{4,132},{6,134},{8,136},{10,138},{12,140},{14,142}... | collective-permute-start | bytes 2949128 | tf_op jit(solution)/shard_map/cond/branch_14_fun/ppermute | solution.py:327
  4.0 1.3 %collective-permute-start.56 = (bf16[2,192,1280]{2,1,0:T(8,128)(2,1)S(1)}, bf16[2,192,1280]{2,1,0:T(8,128)(2,1)}, u32[]{:S(2)}, u32[]{:S(2)}) collective-permute-start(bf16[2,192,1280]{2,1,0:T(8,128)(2,1)S(1)} %get-tuple-element.481.left), channel_id=1, source_target_pairs={{0,64},{2,66},{4,68},{6,70},{8,72},{10,74},{12,76},{14,78},{16,80}... | collective-permute-start | bytes 2949128 | tf_op jit(solution)/shard_map/cond/branch_14_fun/ppermute | solution.py:327
  5.3 2.0 %branch_14_fun.3 = (f32[4,56,192]{2,1,0:T(8,128)}, f32[16,192]{1,0:T(8,128)S(1)}) custom-call(bf16[2,192,1280]{2,1,0:T(8,128)(2,1)S(1)} %get-tuple-element.481.left, f32[8,1280]{1,0:T(8,128)S(1)} %get-tuple-element.482.rows, s32[1,192]{1,0:T(1,128)S(1)} %get-tuple-element.483.labels.refs_2_), custom_call_target="tpu_custom_call" | custom-call | tf_op jit(solution)/shard_map/cond/branch_14_fun/pallas_call | solution.py:29
  7.3 19.4 %all-to-all-start.14 = ((f32[4,56,192]{2,1,0:T(8,128)}), f32[4,56,192]{2,1,0:T(8,128)S(1)}, u32[]{:S(2)}, u32[]{:S(2)}) async-start(f32[4,56,192]{2,1,0:T(8,128)} %get-tuple-element.486), calls=%async_computation.14 | async-start | bytes 458752 | tf_op jit(solution)/shard_map/cond/branch_14_fun/all_to_all | solution.py:340
  26.6 1.9 %collective-permute-start.59 = (f32[16,192]{1,0:T(8,128)S(1)}, f32[16,192]{1,0:T(8,128)}, u32[]{:S(2)}, u32[]{:S(2)}) collective-permute-start(f32[16,192]{1,0:T(8,128)S(1)} %get-tuple-element.484), channel_id=1, source_target_pairs={{0,128},{4,132},{8,136},{12,140},{16,144},{20,148},{24,152},{28,15... | collective-permute-start | bytes 36872 | tf_op jit(solution)/shard_map/cond/branch_14_fun/ppermute | solution.py:339
  28.5 1.9 %collective-permute-start.58 = (f32[16,192]{1,0:T(8,128)S(1)}, f32[16,192]{1,0:T(8,128)}, u32[]{:S(2)}, u32[]{:S(2)}) collective-permute-start(f32[16,192]{1,0:T(8,128)S(1)} %get-tuple-element.484), channel_id=1, source_target_pairs={{0,64},{4,68},{8,72},{12,76},{16,80},{20,84},{24,88},{28,92},{32,9... | collective-permute-start | bytes 36872 | tf_op jit(solution)/shard_map/cond/branch_14_fun/ppermute | solution.py:339
  30.5 2.5 %all-to-all-done.14.refs_1_ = f32[4,56,192]{2,1,0:T(8,128)S(1)} async-done(((f32[4,56,192]{2,1,0:T(8,128)}), f32[4,56,192]{2,1,0:T(8,128)S(1)}, u32[]{:S(2)}, u32[]{:S(2)}) %all-to-all-start.14) | async-done | bytes 172064 | tf_op jit(solution)/shard_map/cond/branch_14_fun/all_to_all | solution.py:340
  33.0 0.4 branch_14_fun.4
  33.4 24.5 %collective-permute-done.59 = f32[16,192]{1,0:T(8,128)} collective-permute-done((f32[16,192]{1,0:T(8,128)S(1)}, f32[16,192]{1,0:T(8,128)}, u32[]{:S(2)}, u32[]{:S(2)}) %collective-permute-start.59) | collective-permute-done | bytes 12320 | tf_op jit(solution)/shard_map/cond/branch_14_fun/ppermute | solution.py:339
  57.9 0.0 collective-permute-done.58
  57.9 0.0 collective-permute-done.57
  57.9 0.0 collective-permute-done.56
  58.3 2.9 %shard_map.65 = (f32[2,192,192]{2,1,0:T(8,128)S(1)}, f32[96,384]{1,0:T(8,128)S(1)}, f32[96,384]{1,0:T(8,128)S(1)}) custom-call(bf16[2,192,1280]{2,1,0:T(8,128)(2,1)} %get-tuple-element.643.first, bf16[2,192,1280]{2,1,0:T(8,128)(2,1)} %get-tuple-element.644.second, f32[8,1280]{1,0:T(8,128)S(1)} %get-tuple-element.641.rows, ...), custom_call_target="tpu_custom_call" | custom-call | tf_op jit(solution)/shard_map/pallas_call | solution.py:29
  61.2 15.3 %conditional.3 = (f32[4,56,384]{2,1,0:T(8,128)}) conditional(s32[]{:T(128)} %bitcast.1, (f32[2,192,192]{2,1,0:T(8,128)S(1)}, f32[16,192]{1,0:T(8,128)}, f32[16,192]{1,0:T(8,128)}) %tuple.153, (f32[2,192,192]{2,1,0:T(8,128)S(1)}, f32[16,192]{1,0:T(8,128)}, f32[16,192]{1,0:T(8,128)}) %tuple.153, ...), branch_computations={%region_21.0_spmd, %region_22.0_spmd, %region_23.0_spmd, %region_2... | conditional | bytes 1179736 | solution.py:386
  61.3 3.2 %collective-permute-start.97 = (f32[96,384]{1,0:T(8,128)S(1)}, f32[96,384]{1,0:T(8,128)S(1)}, u32[]{:S(2)}, u32[]{:S(2)}) collective-permute-start(f32[96,384]{1,0:T(8,128)S(1)} %get-tuple-element.595), channel_id=1, source_target_pairs={{64,0},{66,2},{68,4},{70,6},{72,8},{74,10},{76,12},{78,14},{80,16}... | collective-permute-start | bytes 442376 | tf_op jit(solution)/shard_map/cond/branch_14_fun/ppermute | solution.py:361
  64.5 8.2 %collective-permute-start.98 = (f32[96,384]{1,0:T(8,128)S(1)}, f32[96,384]{1,0:T(8,128)S(1)}, u32[]{:S(2)}, u32[]{:S(2)}) collective-permute-start(f32[96,384]{1,0:T(8,128)S(1)} %get-tuple-element.596), channel_id=1, source_target_pairs={{128,0},{130,2},{132,4},{134,6},{136,8},{138,10},{140,12},{142,14}... | collective-permute-start | bytes 442376 | tf_op jit(solution)/shard_map/cond/branch_14_fun/ppermute | solution.py:361
  72.8 0.0 collective-permute-done.97.refs_3_
  72.8 2.1 %collective-permute-done.98.refs_4_ = f32[96,384]{1,0:T(8,128)S(1)} collective-permute-done((f32[96,384]{1,0:T(8,128)S(1)}, f32[96,384]{1,0:T(8,128)S(1)}, u32[]{:S(2)}, u32[]{:S(2)}) %collective-permute-start.98) | collective-permute-done | bytes 147488 | tf_op jit(solution)/shard_map/cond/branch_14_fun/ppermute | solution.py:361
  74.9 1.7 %branch_14_fun.5 = f32[4,56,384]{2,1,0:T(8,128)} custom-call(f32[2,192,192]{2,1,0:T(8,128)S(1)} %get-tuple-element.592.refs_0_, f32[16,192]{1,0:T(8,128)} %get-tuple-element.593.refs_1_, f32[16,192]{1,0:T(8,128)} %get-tuple-element.594.refs_2_, f32[96,384]{1,0:T(8,128)S(1)} %collective-permute-done.97.refs_3_, f32[96,384]{1,0:T(8,128)S(1)} %collective-permute-done.98.refs_4_), custom_call_target="tpu_custom_call" | custom-call | tf_op jit(solution)/shard_map/cond/branch_14_fun/pallas_call | solution.py:29
  76.5 4.2 %all-to-all-start.21 = ((f32[4,56,384]{2,1,0:T(8,128)}), f32[4,56,384]{2,1,0:T(8,128)S(1)}, u32[]{:S(2)}, u32[]{:S(2)}) async-start(f32[4,56,384]{2,1,0:T(8,128)} %get-tuple-element.778), calls=%async_computation.21 | async-start | bytes 688128 | tf_op jit(solution)/shard_map/all_to_all | solution.py:395
  80.8 1.1 %shard_map.66.refs_3_ = f32[3,48,192]{2,1,0:T(8,128)S(1)} custom-call(s32[1]{0:T(128)} %bitcast.refs_0_.refs_1_, f32[8,192]{1,0:T(8,128)S(1)} %get-tuple-element.650.refs_1_, s32[1,192]{1,0:T(1,128)S(1)} %get-tuple-element.642.refs_2_.refs_4_, f32[16,192]{1,0:T(8,128)} %get-tuple-element.646.refs_3_, f32[16,192]{1,0:T(8,128)} %get-tuple-element.647.refs_4_, ...), custom_call_target="tpu_custom_call" | custom-call | tf_op jit(solution)/shard_map/pallas_call | solution.py:29
  81.9 6.5 %all-to-all-done.21.refs_2_ = f32[4,56,384]{2,1,0:T(8,128)S(1)} async-done(((f32[4,56,384]{2,1,0:T(8,128)}), f32[4,56,384]{2,1,0:T(8,128)S(1)}, u32[]{:S(2)}, u32[]{:S(2)}) %all-to-all-start.21) | async-done | bytes 344096 | tf_op jit(solution)/shard_map/all_to_all | solution.py:395
  88.3 1.9 %shard_map.67 = f32[3,48,192]{2,1,0:T(8,128)} custom-call(s32[1]{0:T(128)} %get-tuple-element.638.refs_0_, s32[1]{0:T(128)} %bitcast.refs_0_.refs_1_, f32[4,56,384]{2,1,0:T(8,128)S(1)} %all-to-all-done.21.refs_2_, f32[3,48,192]{2,1,0:T(8,128)S(1)} %shard_map.66.refs_3_, s32[1,192]{1,0:T(1,128)S(1)} %get-tuple-element.642.refs_2_.refs_4_), custom_call_target="tpu_custom_call" | custom-call | tf_op jit(solution)/shard_map/pallas_call | solution.py:29
Async XLA Ops:
  2.7 55.2 %collective-permute-start.57 = (bf16[2,192,1280]{2,1,0:T(8,128)(2,1)S(1)}, bf16[2,192,1280]{2,1,0:T(8,128)(2,1)}, u32[]{:S(2)}, u32[]{:S(2)}) collective-permute-start(bf16[2,192,1280]{2,1,0:T(8,128)(2,1)S(1)} %get-tuple-element.481.left), channel_id=1, source_target_pairs={{0,128},{2,130},{4,132},{6,134},{8,136},{10,138},{12,140},{14,142}... | collective-permute-start | bytes 2949128 | tf_op jit(solution)/shard_map/cond/branch_14_fun/ppermute | solution.py:327
  4.0 53.9 %collective-permute-start.56 = (bf16[2,192,1280]{2,1,0:T(8,128)(2,1)S(1)}, bf16[2,192,1280]{2,1,0:T(8,128)(2,1)}, u32[]{:S(2)}, u32[]{:S(2)}) collective-permute-start(bf16[2,192,1280]{2,1,0:T(8,128)(2,1)S(1)} %get-tuple-element.481.left), channel_id=1, source_target_pairs={{0,64},{2,66},{4,68},{6,70},{8,72},{10,74},{12,76},{14,78},{16,80}... | collective-permute-start | bytes 2949128 | tf_op jit(solution)/shard_map/cond/branch_14_fun/ppermute | solution.py:327
  7.3 25.7 %all-to-all-start.14 = ((f32[4,56,192]{2,1,0:T(8,128)}), f32[4,56,192]{2,1,0:T(8,128)S(1)}, u32[]{:S(2)}, u32[]{:S(2)}) async-start(f32[4,56,192]{2,1,0:T(8,128)} %get-tuple-element.486), calls=%async_computation.14 | async-start | bytes 458752 | tf_op jit(solution)/shard_map/cond/branch_14_fun/all_to_all | solution.py:340
  26.6 31.2 %collective-permute-start.59 = (f32[16,192]{1,0:T(8,128)S(1)}, f32[16,192]{1,0:T(8,128)}, u32[]{:S(2)}, u32[]{:S(2)}) collective-permute-start(f32[16,192]{1,0:T(8,128)S(1)} %get-tuple-element.484), channel_id=1, source_target_pairs={{0,128},{4,132},{8,136},{12,140},{16,144},{20,148},{24,152},{28,15... | collective-permute-start | bytes 36872 | tf_op jit(solution)/shard_map/cond/branch_14_fun/ppermute | solution.py:339
  28.5 29.3 %collective-permute-start.58 = (f32[16,192]{1,0:T(8,128)S(1)}, f32[16,192]{1,0:T(8,128)}, u32[]{:S(2)}, u32[]{:S(2)}) collective-permute-start(f32[16,192]{1,0:T(8,128)S(1)} %get-tuple-element.484), channel_id=1, source_target_pairs={{0,64},{4,68},{8,72},{12,76},{16,80},{20,84},{24,88},{28,92},{32,9... | collective-permute-start | bytes 36872 | tf_op jit(solution)/shard_map/cond/branch_14_fun/ppermute | solution.py:339
  61.3 11.5 %collective-permute-start.97 = (f32[96,384]{1,0:T(8,128)S(1)}, f32[96,384]{1,0:T(8,128)S(1)}, u32[]{:S(2)}, u32[]{:S(2)}) collective-permute-start(f32[96,384]{1,0:T(8,128)S(1)} %get-tuple-element.595), channel_id=1, source_target_pairs={{64,0},{66,2},{68,4},{70,6},{72,8},{74,10},{76,12},{78,14},{80,16}... | collective-permute-start | bytes 442376 | tf_op jit(solution)/shard_map/cond/branch_14_fun/ppermute | solution.py:361
  64.5 10.3 %collective-permute-start.98 = (f32[96,384]{1,0:T(8,128)S(1)}, f32[96,384]{1,0:T(8,128)S(1)}, u32[]{:S(2)}, u32[]{:S(2)}) collective-permute-start(f32[96,384]{1,0:T(8,128)S(1)} %get-tuple-element.596), channel_id=1, source_target_pairs={{128,0},{130,2},{132,4},{134,6},{136,8},{138,10},{140,12},{142,14}... | collective-permute-start | bytes 442376 | tf_op jit(solution)/shard_map/cond/branch_14_fun/ppermute | solution.py:361
  76.5 11.8 %all-to-all-start.21 = ((f32[4,56,384]{2,1,0:T(8,128)}), f32[4,56,384]{2,1,0:T(8,128)S(1)}, u32[]{:S(2)}, u32[]{:S(2)}) async-start(f32[4,56,384]{2,1,0:T(8,128)} %get-tuple-element.778), calls=%async_computation.21 | async-start | bytes 688128 | tf_op jit(solution)/shard_map/all_to_all | solution.py:395

commit v6 on v5

--- a/solution.py
+++ b/solution.py
@@ -194,7 +194,21 @@
     out[...] = summed[0:height, :] * norms(sums, own_labels, slice_sums, slice_labels, total)
 
 
-def pair_kernel(first, second, rows, left, own_out, first_out, second_out, blocks, sems):
+def pair_kernel(
+    first,
+    second,
+    first_partial,
+    second_partial,
+    rows,
+    left,
+    own_out,
+    first_out,
+    second_out,
+    table_out,
+    blocks,
+    tables,
+    sems,
+):
     count = own_out.shape[2]
     copies = [
         [
@@ -205,9 +219,12 @@
         ]
         for t in range(2)
     ]
-    for pair in copies:
-        for copy in pair:
-            copy.start()
+    table_copies = [
+        pltpu.make_async_copy(partial, tables.at[s], sems.at[4 + s])
+        for s, partial in enumerate((first_partial, second_partial))
+    ]
+    for copy in copies[0] + table_copies + copies[1]:
+        copy.start()
     weights = rows[0:1, :].astype(bf16)
     own_sum, sent_sum = None, None
     for t in range(2):
@@ -223,13 +240,15 @@
         sent = sent_sum[count * s : count * (s + 1)].T
         out[:, 0:count] = sent[0:half]
         out[:, count:] = sent[half:]
-
-
-def merge_kernel(whole, own, first_partial, second_partial, *refs):
+        table_copies[s].wait()
+        table_out[:, count * s : count * (s + 1)] = tables[s, 0:class_count, :]
+
+
+def merge_kernel(whole, own, table, *refs):
     received, out = list(refs[:-1]), refs[-1]
     parts, height = out.shape[0], out.shape[1] - class_count
     count = own.shape[2]
-    for s, partial in enumerate((first_partial, second_partial)):
+    for s in range(2):
         back_in = None if whole[s] else received.pop(0)
         across = slice(count * s, count * (s + 1))
         for q in range(parts):
@@ -238,7 +257,8 @@
                 side, at = divmod(q * height, back_in.shape[0])
                 scores += back_in[at : at + height, count * side : count * (side + 1)]
             out[q, 0:height, across] = scores
-            out[q, height:, across] = partial[0:class_count, :]
+    for q in range(parts):
+        out[q, height:, :] = table[...]
 
 
 def left_kernel(total, place, sums, labels, first_partial, second_partial, self_out, out, scratch):
@@ -356,7 +376,7 @@
         def merge_call(*refs):
             merge_kernel(whole, *refs)
 
-        def run(own, first_partial, second_partial, *sent):
+        def run(own, table, *sent):
             received = [
                 lax.ppermute(part, axes, back(one_way(blocks, voxes, bit)))
                 for part, bit, all_sent in zip(sent, bits, whole)
@@ -365,9 +385,9 @@
             return local_call(
                 merge_call,
                 shape((voxes, height + class_count, 2 * count), f32),
-                [in_vmem] * (3 + len(received)),
+                [in_vmem] * (2 + len(received)),
                 in_vmem,
-                (own, first_partial, second_partial, *received),
+                (own, table, *received),
             )
 
         return run
@@ -375,22 +395,22 @@
     first, second, first_partial, second_partial, sums, self_out = lax.switch(
         index, [fetch(bits) for bits in bit_pairs], left, rows, labels, place
     )
-    own, first_sent, second_sent = local_call(
+    own, first_sent, second_sent, table = local_call(
         pair_kernel,
-        (shape((2, count, count), f32),) + (shape((count // 2, 2 * count), f32),) * 2,
-        [in_hbm, in_hbm, in_vmem, in_vmem],
-        (in_vmem,) * 3,
-        (first, second, rows, left),
-        [pltpu.VMEM((2, 2 * count, width), bf16), pltpu.SemaphoreType.DMA((4,))],
+        (shape((2, count, count), f32),)
+        + (shape((count // 2, 2 * count), f32),) * 2
+        + (shape((class_count, 2 * count), f32),),
+        [in_hbm] * 4 + [in_vmem] * 2,
+        (in_vmem,) * 4,
+        (first, second, first_partial, second_partial, rows, left),
+        [
+            pltpu.VMEM((2, 2 * count, width), bf16),
+            pltpu.VMEM((2, 2 * class_count, count), f32),
+            pltpu.SemaphoreType.DMA((6,)),
+        ],
     )
     merged = lax.switch(
-        index,
-        [give_back(bits) for bits in bit_pairs],
-        own,
-        first_partial,
-        second_partial,
-        first_sent,
-        second_sent,
+        index, [give_back(bits) for bits in bit_pairs], own, table, first_sent, second_sent
     )
     pieces = lax.all_to_all(merged, "vox", 0, 0, tiled=True)
     factors = local_call(

time: 91 us -> 104 us (1.14)
  starting transfers between devices: 41.5 us -> 49.9 us
  waiting for transfers between devices: 35.5 us -> 41.4 us
    all_to_all x1, starting transfers between devices: 4.24 us -> 13.5 us  [body(): pieces = lax.all_to_all(merged, 'vox', 0, 0, tiled=True)]
    ppermute x2 -> x1, starting transfers between devices: 11.5 us -> 4.98 us  [run(): lax.ppermute(part, axes, back(one_way(blocks, voxes, bit)))]
    ppermute x2, waiting for transfers between devices: 24.5 us -> 30.4 us  [run(): lax.ppermute(partial, 'blk', both_ways(blocks, bit))]
    ppermute x2, starting transfers between devices: 2.58 us -> 6.95 us  [run(): blocks_in = [lax.ppermute(left, axes, pair) for pair in pairs]]
    all_to_all x1, starting transfers between devices: 19.4 us -> 20.6 us  [run(): message = lax.all_to_all(message, 'vox', 0, 0, tiled=True)]
  transfers between devices with their start and end apart: 8 -> 7, of which waited for: 4 -> 4; matrix products, arithmetic and copies ran while one was open for 0% -> 0% of each run, Pallas kernels for 4% -> 3%
where the time goes in v6:
time: 104 us
  starting transfers between devices  49.9 us (48%)
  waiting for transfers between devices  41.4 us (40%)
  Pallas kernels  11.4 us (11%)
    ppermute x2, waiting for transfers between devices, run(): lax.ppermute(partial, 'blk', both_ways(blocks, bit))  30.4 us
    all_to_all x1, starting transfers between devices, run(): message = lax.all_to_all(message, 'vox', 0, 0, tiled=True)  20.6 us
    all_to_all x1, starting transfers between devices, body(): pieces = lax.all_to_all(merged, 'vox', 0, 0, tiled=True)  13.5 us
    pallas_call x7, Pallas kernels, local_call(): pl.pallas_call(kernel, out_shape=out_shape, in_specs=in_specs, out_specs=...  11.4 us
    ppermute x2, starting transfers between devices, run(): blocks_in = [lax.ppermute(left, axes, pair) for pair in pairs]  6.95 us
    all_to_all x1, waiting for transfers between devices, body(): pieces = lax.all_to_all(merged, 'vox', 0, 0, tiled=True)  6.45 us
    ppermute x1, starting transfers between devices, run(): lax.ppermute(part, axes, back(one_way(blocks, voxes, bit)))  4.98 us
    ppermute x2, starting transfers between devices, run(): lax.ppermute(partial, 'blk', both_ways(blocks, bit))  3.87 us
  transfers between devices with their start and end apart: 7, of which 4 were waited for; matrix products, arithmetic and copies ran while one was open for 0% of the time, Pallas kernels for 3%

profile of v6, /device:TPU:1, one launch (start us, length us, event | category | flops | bytes accessed | tf_op | source)
XLA Modules:
  0.0 103.9 jit_solution(14750266345171287248)
XLA Ops:
  0.0 2.0 %shard_map.64 = (s32[1]{0:T(128)}, s32[1]{0:T(128)}, bf16[2,192,1280]{2,1,0:T(8,128)(2,1)S(1)}, f32[8,1280]{1,0:T(8,128)S(1)}, s32[1,192]{1,0:T(1,128)S(1)}) custom-call(bf16[192,2,1280]{2,1,0:T(2,128)(2,1)} %refs_0_.1, s32[192]{0:T(256)} %refs_1_.1, s32[2,128]{1,0:T(2,128)} %refs_2_.1, s32[1280]{0:T(1024)} %refs_3_.1, s32[1280]{0:T(1024)} %refs_4_.1, f32[13]{0:T(128)} %refs_5_.1), custom_call_target="tpu_custom_call" | custom-call | tf_op jit(solution)/shard_map/pallas_call | solution.py:29
  2.6 67.2 %conditional.2 = (bf16[2,192,1280]{2,1,0:T(8,128)(2,1)}, bf16[2,192,1280]{2,1,0:T(8,128)(2,1)}, f32[16,192]{1,0:T(8,128)}, f32[16,192]{1,0:T(8,128)}, f32[8,192]{1,0:T(8,128)S(1)}, /*index=5*/f32[48,192]{1,0:T(8,128)S(1)}) conditional(s32[]{:T(128)} %bitcast.1, (bf16[2,192,1280]{2,1,0:T(8,128)(2,1)S(1)}, ...), branch_computations={%region_0.0_spmd, %region_1.0_spmd, %region_2.0_spmd, %region_3.0_... | conditional | bytes 8593648 | solution.py:395
  2.9 1.3 %collective-permute-start.69 = (bf16[2,192,1280]{2,1,0:T(8,128)(2,1)S(1)}, bf16[2,192,1280]{2,1,0:T(8,128)(2,1)}, u32[]{:S(2)}, u32[]{:S(2)}) collective-permute-start(bf16[2,192,1280]{2,1,0:T(8,128)(2,1)S(1)} %get-tuple-element.463.left), channel_id=1, source_target_pairs={{0,256},{2,258},{4,260},{6,262},{8,264},{10,266},{12,268},{14,270}... | collective-permute-start | bytes 2949128 | tf_op jit(solution)/shard_map/cond/branch_17_fun/ppermute | solution.py:347
  4.2 5.7 %collective-permute-start.68 = (bf16[2,192,1280]{2,1,0:T(8,128)(2,1)S(1)}, bf16[2,192,1280]{2,1,0:T(8,128)(2,1)}, u32[]{:S(2)}, u32[]{:S(2)}) collective-permute-start(bf16[2,192,1280]{2,1,0:T(8,128)(2,1)S(1)} %get-tuple-element.463.left), channel_id=1, source_target_pairs={{0,16},{1,17},{2,18},{3,19},{4,20},{5,21},{6,22},{7,23},{8,24},{9,... | collective-permute-start | bytes 2949128 | tf_op jit(solution)/shard_map/cond/branch_17_fun/ppermute | solution.py:347
  9.8 2.0 %branch_17_fun.3 = (f32[4,56,192]{2,1,0:T(8,128)}, f32[16,192]{1,0:T(8,128)S(1)}) custom-call(bf16[2,192,1280]{2,1,0:T(8,128)(2,1)S(1)} %get-tuple-element.463.left, f32[8,1280]{1,0:T(8,128)S(1)} %get-tuple-element.464.rows, s32[1,192]{1,0:T(1,128)S(1)} %get-tuple-element.465.labels.refs_2_), custom_call_target="tpu_custom_call" | custom-call | tf_op jit(solution)/shard_map/cond/branch_17_fun/pallas_call | solution.py:29
  11.8 20.6 %all-to-all-start.17 = ((f32[4,56,192]{2,1,0:T(8,128)}), f32[4,56,192]{2,1,0:T(8,128)S(1)}, u32[]{:S(2)}, u32[]{:S(2)}) async-start(f32[4,56,192]{2,1,0:T(8,128)} %get-tuple-element.468), calls=%async_computation.17 | async-start | bytes 458752 | tf_op jit(solution)/shard_map/cond/branch_17_fun/all_to_all | solution.py:360
  32.4 1.9 %collective-permute-start.71 = (f32[16,192]{1,0:T(8,128)S(1)}, f32[16,192]{1,0:T(8,128)}, u32[]{:S(2)}, u32[]{:S(2)}) collective-permute-start(f32[16,192]{1,0:T(8,128)S(1)} %get-tuple-element.466), channel_id=1, source_target_pairs={{0,256},{4,260},{8,264},{12,268},{16,272},{20,276},{24,280},{28,28... | collective-permute-start | bytes 36872 | tf_op jit(solution)/shard_map/cond/branch_17_fun/ppermute | solution.py:359
  34.3 2.0 %collective-permute-start.70 = (f32[16,192]{1,0:T(8,128)S(1)}, f32[16,192]{1,0:T(8,128)}, u32[]{:S(2)}, u32[]{:S(2)}) collective-permute-start(f32[16,192]{1,0:T(8,128)S(1)} %get-tuple-element.466), channel_id=1, source_target_pairs={{0,16},{4,20},{8,24},{12,28},{16,0},{20,4},{24,8},{28,12},{32,48},... | collective-permute-start | bytes 36872 | tf_op jit(solution)/shard_map/cond/branch_17_fun/ppermute | solution.py:359
  36.3 2.4 %all-to-all-done.17.refs_1_ = f32[4,56,192]{2,1,0:T(8,128)S(1)} async-done(((f32[4,56,192]{2,1,0:T(8,128)}), f32[4,56,192]{2,1,0:T(8,128)S(1)}, u32[]{:S(2)}, u32[]{:S(2)}) %all-to-all-start.17) | async-done | bytes 172064 | tf_op jit(solution)/shard_map/cond/branch_17_fun/all_to_all | solution.py:360
  38.7 0.4 branch_17_fun.4
  39.1 30.4 %collective-permute-done.71 = f32[16,192]{1,0:T(8,128)} collective-permute-done((f32[16,192]{1,0:T(8,128)S(1)}, f32[16,192]{1,0:T(8,128)}, u32[]{:S(2)}, u32[]{:S(2)}) %collective-permute-start.71) | collective-permute-done | bytes 12320 | tf_op jit(solution)/shard_map/cond/branch_17_fun/ppermute | solution.py:359
  69.6 0.0 collective-permute-done.70
  69.6 0.0 collective-permute-done.69
  69.6 0.0 collective-permute-done.68
  69.8 3.2 %shard_map.65 = (f32[2,192,192]{2,1,0:T(8,128)S(1)}, f32[96,384]{1,0:T(8,128)S(1)}, f32[96,384]{1,0:T(8,128)S(1)}, f32[8,384]{1,0:T(8,128)S(1)}) custom-call(bf16[2,192,1280]{2,1,0:T(8,128)(2,1)} %get-tuple-element.581.first, bf16[2,192,1280]{2,1,0:T(8,128)(2,1)} %get-tuple-element.582.second, f32[16,192]{1,0:T(8,128)} %get-tuple-element.583.first_partial.refs_3_, ...), custom_call_target="tpu_custom_call" | custom-call | tf_op jit(solution)/shard_map/pallas_call | solution.py:29
  73.0 8.0 %conditional.3 = (f32[4,56,384]{2,1,0:T(8,128)}) conditional(s32[]{:T(128)} %bitcast.1, (f32[2,192,192]{2,1,0:T(8,128)S(1)}, f32[8,384]{1,0:T(8,128)S(1)}) %tuple.153, (f32[2,192,192]{2,1,0:T(8,128)S(1)}, f32[8,384]{1,0:T(8,128)S(1)}) %tuple.153, (f32[96,384]{1,0:T(8,128)S(1)}, f32[96,384]{1,0:T(8,128)S(1)}, ...), branch_computations={%region_21.0_spmd, %region_22.0_spmd, %region_23.0_spmd, %region_2... | conditional | bytes 1179736 | solution.py:412
  73.0 5.0 %collective-permute-start.101 = (f32[96,384]{1,0:T(8,128)S(1)}, f32[96,384]{1,0:T(8,128)S(1)}, u32[]{:S(2)}, u32[]{:S(2)}) collective-permute-start(f32[96,384]{1,0:T(8,128)S(1)} %get-tuple-element.548), channel_id=1, source_target_pairs={{256,0},{258,2},{260,4},{262,6},{264,8},{266,10},{268,12},{270,14}... | collective-permute-start | bytes 442376 | tf_op jit(solution)/shard_map/cond/branch_17_fun/ppermute | solution.py:381
  78.0 2.1 %collective-permute-done.101.refs_2_ = f32[96,384]{1,0:T(8,128)S(1)} collective-permute-done((f32[96,384]{1,0:T(8,128)S(1)}, f32[96,384]{1,0:T(8,128)S(1)}, u32[]{:S(2)}, u32[]{:S(2)}) %collective-permute-start.101) | collective-permute-done | bytes 147488 | tf_op jit(solution)/shard_map/cond/branch_17_fun/ppermute | solution.py:381
  80.1 0.9 branch_17_fun.5
  81.0 13.5 %all-to-all-start.21 = ((f32[4,56,384]{2,1,0:T(8,128)}), f32[4,56,384]{2,1,0:T(8,128)S(1)}, u32[]{:S(2)}, u32[]{:S(2)}) async-start(f32[4,56,384]{2,1,0:T(8,128)} %get-tuple-element.717), calls=%async_computation.21 | async-start | bytes 688128 | tf_op jit(solution)/shard_map/all_to_all | solution.py:415
  94.5 1.1 %shard_map.66.refs_3_ = f32[3,48,192]{2,1,0:T(8,128)S(1)} custom-call(s32[1]{0:T(128)} %bitcast.refs_0_.refs_1_, f32[8,192]{1,0:T(8,128)S(1)} %get-tuple-element.589.refs_1_, s32[1,192]{1,0:T(1,128)S(1)} %get-tuple-element.580.refs_2_.refs_4_, f32[16,192]{1,0:T(8,128)} %get-tuple-element.583.first_partial.refs_3_, ...), custom_call_target="tpu_custom_call" | custom-call | tf_op jit(solution)/shard_map/pallas_call | solution.py:29
  95.6 6.5 %all-to-all-done.21.refs_2_ = f32[4,56,384]{2,1,0:T(8,128)S(1)} async-done(((f32[4,56,384]{2,1,0:T(8,128)}), f32[4,56,384]{2,1,0:T(8,128)S(1)}, u32[]{:S(2)}, u32[]{:S(2)}) %all-to-all-start.21) | async-done | bytes 344096 | tf_op jit(solution)/shard_map/all_to_all | solution.py:415
  102.0 1.9 %shard_map.67 = f32[3,48,192]{2,1,0:T(8,128)} custom-call(s32[1]{0:T(128)} %get-tuple-element.576.refs_0_, s32[1]{0:T(128)} %bitcast.refs_0_.refs_1_, f32[4,56,384]{2,1,0:T(8,128)S(1)} %all-to-all-done.21.refs_2_, f32[3,48,192]{2,1,0:T(8,128)S(1)} %shard_map.66.refs_3_, s32[1,192]{1,0:T(1,128)S(1)} %get-tuple-element.580.refs_2_.refs_4_), custom_call_target="tpu_custom_call" | custom-call | tf_op jit(solution)/shard_map/pallas_call | solution.py:29
Async XLA Ops:
  2.9 66.7 %collective-permute-start.69 = (bf16[2,192,1280]{2,1,0:T(8,128)(2,1)S(1)}, bf16[2,192,1280]{2,1,0:T(8,128)(2,1)}, u32[]{:S(2)}, u32[]{:S(2)}) collective-permute-start(bf16[2,192,1280]{2,1,0:T(8,128)(2,1)S(1)} %get-tuple-element.463.left), channel_id=1, source_target_pairs={{0,256},{2,258},{4,260},{6,262},{8,264},{10,266},{12,268},{14,270}... | collective-permute-start | bytes 2949128 | tf_op jit(solution)/shard_map/cond/branch_17_fun/ppermute | solution.py:347
  4.2 65.4 %collective-permute-start.68 = (bf16[2,192,1280]{2,1,0:T(8,128)(2,1)S(1)}, bf16[2,192,1280]{2,1,0:T(8,128)(2,1)}, u32[]{:S(2)}, u32[]{:S(2)}) collective-permute-start(bf16[2,192,1280]{2,1,0:T(8,128)(2,1)S(1)} %get-tuple-element.463.left), channel_id=1, source_target_pairs={{0,16},{1,17},{2,18},{3,19},{4,20},{5,21},{6,22},{7,23},{8,24},{9,... | collective-permute-start | bytes 2949128 | tf_op jit(solution)/shard_map/cond/branch_17_fun/ppermute | solution.py:347
  11.8 26.9 %all-to-all-start.17 = ((f32[4,56,192]{2,1,0:T(8,128)}), f32[4,56,192]{2,1,0:T(8,128)S(1)}, u32[]{:S(2)}, u32[]{:S(2)}) async-start(f32[4,56,192]{2,1,0:T(8,128)} %get-tuple-element.468), calls=%async_computation.17 | async-start | bytes 458752 | tf_op jit(solution)/shard_map/cond/branch_17_fun/all_to_all | solution.py:360
  32.4 37.2 %collective-permute-start.71 = (f32[16,192]{1,0:T(8,128)S(1)}, f32[16,192]{1,0:T(8,128)}, u32[]{:S(2)}, u32[]{:S(2)}) collective-permute-start(f32[16,192]{1,0:T(8,128)S(1)} %get-tuple-element.466), channel_id=1, source_target_pairs={{0,256},{4,260},{8,264},{12,268},{16,272},{20,276},{24,280},{28,28... | collective-permute-start | bytes 36872 | tf_op jit(solution)/shard_map/cond/branch_17_fun/ppermute | solution.py:359
  34.3 35.2 %collective-permute-start.70 = (f32[16,192]{1,0:T(8,128)S(1)}, f32[16,192]{1,0:T(8,128)}, u32[]{:S(2)}, u32[]{:S(2)}) collective-permute-start(f32[16,192]{1,0:T(8,128)S(1)} %get-tuple-element.466), channel_id=1, source_target_pairs={{0,16},{4,20},{8,24},{12,28},{16,0},{20,4},{24,8},{28,12},{32,48},... | collective-permute-start | bytes 36872 | tf_op jit(solution)/shard_map/cond/branch_17_fun/ppermute | solution.py:359
  73.0 7.1 %collective-permute-start.101 = (f32[96,384]{1,0:T(8,128)S(1)}, f32[96,384]{1,0:T(8,128)S(1)}, u32[]{:S(2)}, u32[]{:S(2)}) collective-permute-start(f32[96,384]{1,0:T(8,128)S(1)} %get-tuple-element.548), channel_id=1, source_target_pairs={{256,0},{258,2},{260,4},{262,6},{264,8},{266,10},{268,12},{270,14}... | collective-permute-start | bytes 442376 | tf_op jit(solution)/shard_map/cond/branch_17_fun/ppermute | solution.py:381
  81.0 21.0 %all-to-all-start.21 = ((f32[4,56,384]{2,1,0:T(8,128)}), f32[4,56,384]{2,1,0:T(8,128)S(1)}, u32[]{:S(2)}, u32[]{:S(2)}) async-start(f32[4,56,384]{2,1,0:T(8,128)} %get-tuple-element.717), calls=%async_computation.21 | async-start | bytes 688128 | tf_op jit(solution)/shard_map/all_to_all | solution.py:415
